TPU v7x, 32 devices: a whole 2x2x4 slice. The times are simulated.
32 devices in a mesh: gs: 8 (over z, y), view: 4 (over x, core).
Axes of the slice: x: 2, y: 2, z: 4, core: 2. Of those that a mesh axis runs over, the one named last changes fastest.
Arguments:
- means: float32 [3, 8192], P(None, 'gs'), may hold values from -256 to 256, as said below
- quats: float32 [4, 8192], P(None, 'gs'), may hold values from -1 to 2, as said below
- log_scales: float32 [3, 8192], P(None, 'gs'), may hold values from -2.6 to -1.6
- opacity: float32 [8192], P('gs'), may hold values from -5.5 to -2.5
- sh_coeffs: float32 [48, 8192], P(None, 'gs'), may hold values from -1.8 to 1.8
- cameras: float32 [4, 2], P('view'), may hold values from -1 to 128
- targets: float32 [4, 3, 128, 128], P('view', None, 'gs'), may hold values from 0 to 1
- send_rows: int32 [8, 8, 128], P('gs'), may hold values from 0 to 1023, as said below
- tile_lists: int32 [4, 8, 8, 128], P('view', 'gs'), may hold values from 0 to 1023, as said below
- list_lengths: int32 [4, 8, 8], P('view', 'gs'), may hold values from 0 to 128
Outputs:
- rendered: float32 [4, 3, 128, 128], P('view', None, 'gs')
- grad_means: float32 [3, 8192], P(None, 'gs')
- grad_quats: float32 [4, 8192], P(None, 'gs')
- grad_log_scales: float32 [3, 8192], P(None, 'gs')
- grad_opacity: float32 [8192], P('gs')
- grad_sh: float32 [48, 8192], P(None, 'gs')
Inputs may be any that keep to these rules, and one draw needn't show every extreme that they name: `send_rows`: slots k of a pair (source, owner) below that pair's count hold distinct rows, each row in at most one used slot of its source; every source fills all 128 slots of one owner. `tile_lists`: the used entries of a list are distinct used slots in increasing depth. `quats`: the real part lies in 1 to 2, the others in -1 to 1. `means`: depths lie in 10 to 10.5.
All inputs are finite; a program needn't handle non-finite values.
Results may differ from a plain program's by a relative error of at most 0.0003.
Values sent between devices are 32-bit elements; how exact they have to be, the bound alone decides.
A program may use at most 64 MiB of HBM per device.

v0:
```python
import math

import jax
import jax.numpy as jnp
from jax import lax
from jax.experimental import pallas as pl
from jax.experimental.pallas import tpu as pltpu
from jax.sharding import PartitionSpec as P

TILE = 16
SH = 16
RADIUS = 5
LANES = 128
ROWS_MSG = 16
VMEM = pltpu.VMEM
MESH = pl.DeviceIdType.MESH

focal_length = 1000.0
cov_blur = 0.3
ssim_weight = 0.2
charb_eps = 0.0001
ssim_one = 0.0001
ssim_two = 0.0009
sh_c0 = 0.28209479177387814
sh_c1 = 0.4886025119029199
sh_c2 = [
    1.0925484305920792,
    -1.0925484305920792,
    0.31539156525252005,
    -1.0925484305920792,
    0.5462742152960396,
]
sh_c3 = [
    -0.5900435899266435,
    2.890611442640554,
    -0.4570457994644658,
    0.3731763325901154,
    -0.4570457994644658,
    1.445305721320277,
    -0.5900435899266435,
]

f32 = jnp.float32
bf16 = jnp.bfloat16


def sh_basis(dir_x, dir_y, dir_z):
    sq_x = dir_x * dir_x
    sq_y = dir_y * dir_y
    sq_z = dir_z * dir_z
    return [
        None,
        -sh_c1 * dir_y,
        sh_c1 * dir_z,
        -sh_c1 * dir_x,
        sh_c2[0] * dir_x * dir_y,
        sh_c2[1] * dir_y * dir_z,
        sh_c2[2] * (2.0 * sq_z - sq_x - sq_y),
        sh_c2[3] * dir_x * dir_z,
        sh_c2[4] * (sq_x - sq_y),
        sh_c3[0] * dir_y * (3.0 * sq_x - sq_y),
        sh_c3[1] * dir_x * dir_y * dir_z,
        sh_c3[2] * dir_y * (4.0 * sq_z - sq_x - sq_y),
        sh_c3[3] * dir_z * (2.0 * sq_z - 3.0 * sq_x - 3.0 * sq_y),
        sh_c3[4] * dir_x * (4.0 * sq_z - sq_x - sq_y),
        sh_c3[5] * dir_z * (sq_x - sq_y),
        sh_c3[6] * dir_x * (sq_x - 3.0 * sq_y),
    ]


def project(means, quats, log_scales, opacity, coeffs, cameras, centre_x, centre_y):
    inv_norm = 1.0 / jnp.sqrt(
        quats[0] * quats[0] + quats[1] * quats[1] + quats[2] * quats[2] + quats[3] * quats[3]
    )
    quat_w, quat_x, quat_y, quat_z = [quat * inv_norm for quat in quats]
    scales = [jnp.exp(log_scale) for log_scale in log_scales]
    rotation = [
        [
            1.0 - 2.0 * (quat_y * quat_y + quat_z * quat_z),
            2.0 * (quat_x * quat_y - quat_w * quat_z),
            2.0 * (quat_x * quat_z + quat_w * quat_y),
        ],
        [
            2.0 * (quat_x * quat_y + quat_w * quat_z),
            1.0 - 2.0 * (quat_x * quat_x + quat_z * quat_z),
            2.0 * (quat_y * quat_z - quat_w * quat_x),
        ],
        [
            2.0 * (quat_x * quat_z - quat_w * quat_y),
            2.0 * (quat_y * quat_z + quat_w * quat_x),
            1.0 - 2.0 * (quat_x * quat_x + quat_y * quat_y),
        ],
    ]
    spread = [[rotation[i][j] * scales[j] for j in range(3)] for i in range(3)]
    depth_z = means[2]
    inv_depth = 1.0 / depth_z
    jac_diag = focal_length * inv_depth
    diag_top = [jac_diag * spread[0][j] for j in range(3)]
    diag_low = [jac_diag * spread[1][j] for j in range(3)]
    log_alpha = -jnp.log(1.0 + jnp.exp(-opacity))
    views = []
    for cam_x, cam_y in cameras:
        rel_x = means[0] - cam_x
        rel_y = means[1] - cam_y
        ratio_u = jac_diag * rel_x
        ratio_v = jac_diag * rel_y
        jac_u = -ratio_u * inv_depth
        jac_v = -ratio_v * inv_depth
        top = [diag_top[j] + jac_u * spread[2][j] for j in range(3)]
        low = [diag_low[j] + jac_v * spread[2][j] for j in range(3)]
        cov_a = top[0] * top[0] + top[1] * top[1] + top[2] * top[2] + cov_blur
        cov_b = top[0] * low[0] + top[1] * low[1] + top[2] * low[2]
        cov_c = low[0] * low[0] + low[1] * low[1] + low[2] * low[2] + cov_blur
        inv_det = 1.0 / (cov_a * cov_c - cov_b * cov_b)
        inv_dist = 1.0 / jnp.sqrt(rel_x * rel_x + rel_y * rel_y + depth_z * depth_z)
        basis = sh_basis(rel_x * inv_dist, rel_y * inv_dist, depth_z * inv_dist)
        colours = []
        for channel in range(3):
            total = sh_c0 * coeffs[channel * SH] + 0.5
            for k in range(1, SH):
                total = total + coeffs[channel * SH + k] * basis[k]
            colours.append(jnp.maximum(total, 0.0))
        views.append(
            [
                ratio_u + centre_x,
                ratio_v + centre_y,
                cov_c * inv_det,
                -cov_b * inv_det,
                cov_a * inv_det,
                log_alpha,
            ]
            + colours
        )
    return views


def window_taps():
    raw_taps = [math.exp(-((tap_idx - RADIUS) ** 2) / 4.5) for tap_idx in range(2 * RADIUS + 1)]
    total = sum(raw_taps)
    return [tap / total for tap in raw_taps]


def band(out_count, in_count, offset):
    taps = window_taps()
    shape = (out_count, in_count)
    gap = lax.broadcasted_iota(jnp.int32, shape, 1) - lax.broadcasted_iota(jnp.int32, shape, 0)
    gap = jnp.abs(gap - offset)
    matrix = jnp.zeros(shape, f32)
    for far in range(RADIUS + 1):
        matrix = jnp.where(gap == far, taps[RADIUS + far], matrix)
    return matrix


def pieces(x, count):
    out = []
    for _ in range(count - 1):
        part = x.astype(bf16).astype(f32)
        out.append(part)
        x = x - part
    out.append(x)
    return out


def stack(x, count, axis=0):
    return jnp.concatenate(pieces(x, count), axis=axis).astype(bf16)


def dot(a, b):
    return lax.dot_general(a, b, (((1,), (0,)), ((), ())), preferred_element_type=f32)


def dot_t(a, b):
    return lax.dot_general(a, b, (((1,), (1,)), ((), ())), preferred_element_type=f32)


def dot_exact(a, b):
    return lax.dot_general(
        a, b, (((1,), (0,)), ((), ())), precision=lax.Precision.HIGHEST, preferred_element_type=f32
    )


def fold(x, count):
    size = x.shape[0] // count
    total = x[:size]
    for i in range(1, count):
        total = total + x[i * size : (i + 1) * size]
    return total


def loop(low, high, step):
    if high - low <= 8:
        for i in range(low, high):
            step(i)
    else:

        @pl.loop(low, high)
        def _(i):
            step(i)


def params(par, opacity):
    return (
        [par[:, 48 + i, :] for i in range(3)],
        [par[:, 56 + i, :] for i in range(4)],
        [par[:, 64 + i, :] for i in range(3)],
        opacity[...],
        [par[:, i, :] for i in range(48)],
    )


def pick_of(send, d, shard):
    local_row = lax.broadcasted_iota(jnp.int32, (shard, send.shape[2]), 0)
    return jnp.where(local_row == send[0, pl.ds(d, 1), :], 1.0, 0.0).astype(bf16)


def train_kernel(
    n_gs,
    n_view,
    means_in,
    quats_in,
    scales_in,
    opacity_in,
    sh_in,
    camera_in,
    targets_in,
    send_in,
    lists_in,
    lens_in,
    pic_out,
    views_out,
    par,
    opacity,
    send,
    means,
    quats,
    scales,
    sh,
    camera,
    targets,
    lists,
    lens,
    row_buf,
    msg_out,
    msg_in,
    tile_buf,
    ratio_buf,
    weight_buf,
    pic,
    halo,
    t_halo,
    cot,
    back_out,
    back_in,
    placed,
    load_sems,
    send_one,
    recv_one,
    send_halo,
    recv_halo,
    send_tgt,
    recv_tgt,
    send_two,
    recv_two,
    send_three,
    recv_three,
):
    loads = [
        pltpu.make_async_copy(src, dst, load_sems.at[k])
        for k, (src, dst) in enumerate(
            [
                (sh_in, sh),
                (means_in, means),
                (quats_in, quats),
                (scales_in, scales),
                (opacity_in, opacity),
                (camera_in, camera),
                (send_in, send),
                (targets_in, targets),
                (lists_in.at[0, 0], lists),
                (lens_in.at[0], lens),
            ]
        )
    ]
    for load in loads:
        load.start()
    gs = lax.axis_index("gs")
    view = lax.axis_index("view")
    chunks = means.shape[1] // LANES
    cap = send.shape[2]
    shard = means.shape[1]
    tiles = lists.shape[0]
    list_size = lists.shape[1]
    has_up = gs > 0
    has_down = gs < n_gs - 1

    barrier = pltpu.get_barrier_semaphore()

    def greet(strip, cam):
        pl.semaphore_signal(barrier, inc=1, device_id=(strip, cam), device_id_type=MESH)

    loop(1, n_gs, lambda k: greet(lax.rem(gs + k, n_gs), view))
    loop(1, n_view, lambda k: greet(gs, lax.rem(view + k, n_view)))

    for load in loads:
        load.wait()

    for c in range(chunks):
        cols = slice(c * LANES, (c + 1) * LANES)
        par[c, 0:48, :] = sh[:, cols]
        par[c, 48:51, :] = means[:, cols]
        par[c, 56:60, :] = quats[:, cols]
        par[c, 64:67, :] = scales[:, cols]

    centre_x = 0.5 * tiles * TILE
    centre_y = 0.5 * n_gs * TILE
    cam_x = camera[0:1, 0:1]
    cam_y = camera[0:1, 1:2]
    rows = project(*params(par, opacity), [(cam_x, cam_y)], centre_x, centre_y)[0]
    row_buf[...] = jnp.zeros_like(row_buf)
    for i in range(9):
        row_buf[:, i, :] = rows[i]
    table = stack(jnp.concatenate([row_buf[c] for c in range(chunks)], axis=1), 3)

    def fill(d):
        msg_out[d] = fold(dot(table, pick_of(send, d, shard)), 3)

    def first_copy(d, s):
        return pltpu.make_async_remote_copy(
            src_ref=msg_out.at[d],
            dst_ref=msg_in.at[s],
            send_sem=send_one.at[d],
            recv_sem=recv_one.at[s],
            device_id=(d, view),
            device_id_type=MESH,
        )

    pl.semaphore_wait(barrier, n_gs + n_view - 2)

    def send_first(k):
        d = lax.rem(gs + k, n_gs)
        fill(d)
        first_copy(d, gs).start()

    loop(1, n_gs, send_first)
    fill(gs)
    msg_in[gs] = msg_out[gs]

    def halo_copy(src, dst, sends, recvs, side):
        other = gs + 1 if side == 0 else gs - 1
        return pltpu.make_async_remote_copy(
            src_ref=src,
            dst_ref=dst.at[side],
            send_sem=sends.at[side],
            recv_sem=recvs.at[side],
            device_id=(other, view),
            device_id_type=MESH,
        )

    def exchange(src, dst, sends, recvs, start):
        def act(copy, recv):
            if start:
                if not recv:
                    copy.start()
            elif recv:
                copy.wait_recv()
            else:
                copy.wait_send()

        for recv in (False, True):
            if start and recv:
                continue

            @pl.when(has_down)
            def _():
                act(halo_copy(src, dst, sends, recvs, 1 if recv else 0), recv)

            @pl.when(has_up)
            def _():
                act(halo_copy(src, dst, sends, recvs, 0 if recv else 1), recv)

    exchange(targets.at[0], t_halo, send_tgt, recv_tgt, True)

    @pl.when(jnp.logical_not(has_up))
    def _():
        halo[0] = jnp.zeros_like(halo[0])
        t_halo[0] = jnp.zeros_like(t_halo[0])

    @pl.when(jnp.logical_not(has_down))
    def _():
        halo[1] = jnp.zeros_like(halo[1])
        t_halo[1] = jnp.zeros_like(t_halo[1])


    slot_row = lax.broadcasted_iota(jnp.int32, (cap, list_size), 0)

    def slot_pick(s, t):
        return jnp.where(slot_row + s * cap == lists[t : t + 1, :], 1.0, 0.0).astype(bf16)

    tile_buf[...] = jnp.zeros_like(tile_buf)

    def gather(s):
        got = stack(msg_in[s], 3)
        for t in range(tiles):
            tile_buf[t] += fold(dot(got, slot_pick(s, t)), 3)

    gather(gs)

    def gather_next(k):
        s = lax.rem(gs + n_gs - k, n_gs)
        first_copy(gs, s).wait_recv()
        gather(s)

    loop(1, n_gs, gather_next)

    diagonal = lax.broadcasted_iota(jnp.int32, (tiles, tiles), 0) == lax.broadcasted_iota(
        jnp.int32, (tiles, tiles), 1
    )
    used = jnp.sum(jnp.where(diagonal, lens[...].astype(f32), 0.0), axis=1, keepdims=True)
    entry = lax.broadcasted_iota(jnp.int32, (tiles, list_size), 1)
    live = entry.astype(f32) < used
    mid_q = (lax.broadcasted_iota(jnp.int32, (tiles, list_size), 0) * TILE + TILE // 2).astype(f32)
    mid_r = (gs * TILE + TILE // 2).astype(f32)
    off_u = tile_buf[:, 0, :] - mid_q
    off_w = tile_buf[:, 1, :] - mid_r
    k0 = tile_buf[:, 2, :]
    k1 = tile_buf[:, 3, :]
    k2 = tile_buf[:, 4, :]
    lin_u = k0 * off_u + k1 * off_w
    lin_w = k2 * off_w + k1 * off_u
    terms = [
        jnp.where(live, tile_buf[:, 5, :] - 0.5 * (off_u * lin_u + off_w * lin_w), -10000.0),
        jnp.where(live, lin_u, 0.0),
        jnp.where(live, lin_w, 0.0),
        jnp.where(live, -0.5 * k0, 0.0),
        jnp.where(live, -k1, 0.0),
        jnp.where(live, -0.5 * k2, 0.0),
    ]
    term_t = jnp.transpose(jnp.concatenate(pieces(jnp.concatenate(terms, axis=0), 3), axis=0))
    term_t = term_t.astype(bf16)
    colour = jnp.concatenate([tile_buf[:, 6 + c, :] for c in range(3)], axis=0)
    col_hi, col_lo = pieces(colour, 2)
    col_two = jnp.concatenate([col_hi, col_lo], axis=0)
    col_wide = jnp.concatenate([col_two, col_two], axis=1).astype(bf16)
    col_t = jnp.transpose(jnp.concatenate([col_hi, col_lo, col_hi], axis=0)).astype(bf16)

    n_chunk, _, wide = weight_buf.shape
    width = tiles * TILE
    lane = lax.broadcasted_iota(jnp.int32, (tiles, wide), 1)
    in_tile = lax.rem(lane, width) // TILE == lax.broadcasted_iota(jnp.int32, (tiles, wide), 0)

    off_q = (lax.rem(lane, TILE) - TILE // 2).astype(f32)
    half_r = (lane // width).astype(f32)

    def basis(i):
        off_r = half_r + float(i * (wide // width) - TILE // 2)
        out = [jnp.ones_like(off_q), off_q, off_r, off_q * off_q, off_q * off_r, off_r * off_r]
        return jnp.concatenate([jnp.where(in_tile, x, 0.0) for x in out], axis=0).astype(bf16)

    shape = (list_size, 2 * list_size)
    list_row = lax.broadcasted_iota(jnp.int32, shape, 0)
    list_col = lax.rem(lax.broadcasted_iota(jnp.int32, shape, 1), list_size)
    prefix = jnp.where(list_col < list_row, 1.0, 0.0).astype(bf16)
    suffix = jnp.where(list_col > list_row, 1.0, 0.0).astype(bf16)

    for i in range(n_chunk):
        base = basis(i)
        alpha = jnp.exp(dot(term_t, jnp.concatenate([base, base, base], axis=0)))
        keep = 1.0 - alpha
        weight = alpha * jnp.exp(dot(prefix, stack(jnp.log(keep), 2)))
        ratio_buf[i] = alpha / keep
        weight_buf[i] = weight
        drawn = fold(dot(col_wide, stack(weight, 2)), 2)
        for c in range(3):
            mine = jnp.where(in_tile, drawn[c * tiles : (c + 1) * tiles], 0.0)
            line = jnp.sum(mine, axis=0, keepdims=True)
            for half in range(wide // width):
                row = i * (wide // width) + half
                pic[c, row : row + 1, :] = line[:, half * width : (half + 1) * width]

    exchange(pic, halo, send_halo, recv_halo, True)
    pic_out[0] = pic[...]
    exchange(targets.at[0], t_halo, send_tgt, recv_tgt, False)
    exchange(pic, halo, send_halo, recv_halo, False)

    tall = 2 * TILE
    across = band(width, width, 0)
    stacked = []
    images = []
    for c in range(3):
        img = jnp.concatenate([halo[0, c], pic[c], halo[1, c]], axis=0)
        tgt = jnp.concatenate([t_halo[0, c], targets[0, c], t_halo[1, c]], axis=0)
        images.append((img, tgt))
        stacked += [img, tgt, img * img, tgt * tgt, img * tgt]
    down = dot_exact(band(tall, 3 * TILE, TILE // 2), jnp.concatenate(stacked, axis=1))
    down = jnp.concatenate([down[:, i * width : (i + 1) * width] for i in range(15)], axis=0)
    blurred = dot_exact(down, across)
    at_row = lax.broadcasted_iota(jnp.int32, (tall, width), 0) + gs * TILE - TILE // 2
    inside = jnp.logical_and(at_row >= 0, at_row < n_gs * TILE)
    scale = -ssim_weight / (TILE * TILE)
    cots = []
    for c in range(3):
        mean_x, mean_y, raw_xx, raw_yy, raw_xy = [
            blurred[(5 * c + i) * tall : (5 * c + i + 1) * tall] for i in range(5)
        ]
        top_a = 2.0 * mean_x * mean_y + ssim_one
        top_b = 2.0 * (raw_xy - mean_x * mean_y) + ssim_two
        low_c = mean_x * mean_x + mean_y * mean_y + ssim_one
        low_d = (raw_xx - mean_x * mean_x) + (raw_yy - mean_y * mean_y) + ssim_two
        inv_cd = 1.0 / (low_c * low_d)
        inv_dd = inv_cd * low_c
        ssim = top_a * top_b * inv_cd
        d_mean = 2.0 * mean_y * (top_b - top_a) * inv_cd - 2.0 * mean_x * ssim * (
            inv_cd * low_d - inv_dd
        )
        d_xx = -ssim * inv_dd
        d_xy = 2.0 * top_a * inv_cd
        cots += [jnp.where(inside, scale * part, 0.0) for part in (d_mean, d_xx, d_xy)]
    spread = dot_exact(band(TILE, tall, TILE // 2), jnp.concatenate(cots, axis=1))
    spread = jnp.concatenate([spread[:, i * width : (i + 1) * width] for i in range(9)], axis=0)
    spread = dot_exact(spread, across)
    grad_rows = []
    for c in range(3):
        img = pic[c]
        tgt = targets[0, c]
        s_mean, s_xx, s_xy = [spread[(3 * c + i) * TILE : (3 * c + i + 1) * TILE] for i in range(3)]
        res = img - tgt
        direct = (1.0 - ssim_weight) / (TILE * TILE) * res / jnp.sqrt(res * res + charb_eps)
        grad_rows.append(direct + s_mean + 2.0 * img * s_xx + tgt * s_xy)

    d_terms = jnp.zeros((6 * tiles, list_size), f32)
    d_colour = jnp.zeros((3 * tiles, list_size), f32)
    for i in range(n_chunk):
        per = wide // width
        parts = []
        for c in range(3):
            line = jnp.concatenate(
                [grad_rows[c][i * per + half : i * per + half + 1] for half in range(per)], axis=1
            )
            parts.append(jnp.where(in_tile, line, 0.0))
        hi, lo = pieces(jnp.concatenate(parts, axis=0), 2)
        shade = dot(col_t, jnp.concatenate([hi, hi, lo], axis=0).astype(bf16))
        weight = weight_buf[i]
        share = weight * shade
        d_power = share - ratio_buf[i] * dot(suffix, stack(share, 2))
        both = dot_t(basis(i), stack(d_power, 2))
        d_terms = d_terms + both[:, :list_size] + both[:, list_size:]
        both = fold(dot_t(jnp.concatenate([hi, lo], axis=0).astype(bf16), stack(weight, 2)), 2)
        d_colour = d_colour + both[:, :list_size] + both[:, list_size:]

    d0, d1, d2, d3, d4, d5 = [d_terms[k * tiles : (k + 1) * tiles] for k in range(6)]
    e1 = d1 - off_u * d0
    e2 = d2 - off_w * d0
    cot[...] = jnp.zeros_like(cot)
    cot[:, 0, :] = k0 * e1 + k1 * e2
    cot[:, 1, :] = k2 * e2 + k1 * e1
    cot[:, 2, :] = -0.5 * d3 + off_u * (d1 - 0.5 * off_u * d0)
    cot[:, 3, :] = off_w * e1 + off_u * d2 - d4
    cot[:, 4, :] = -0.5 * d5 + off_w * (d2 - 0.5 * off_w * d0)
    cot[:, 5, :] = d0
    for c in range(3):
        cot[:, 6 + c, :] = d_colour[c * tiles : (c + 1) * tiles]
    cot_pieces = [stack(cot[t], 3) for t in range(tiles)]

    def scatter(s):
        total = jnp.zeros((3 * ROWS_MSG, cap), f32)
        for t in range(tiles):
            total = total + dot_t(cot_pieces[t], slot_pick(s, t))
        back_out[s] = fold(total, 3)

    def second_copy(d, s):
        return pltpu.make_async_remote_copy(
            src_ref=back_out.at[d],
            dst_ref=back_in.at[s],
            send_sem=send_two.at[d],
            recv_sem=recv_two.at[s],
            device_id=(d, view),
            device_id_type=MESH,
        )

    def send_second(k):
        d = lax.rem(gs + k, n_gs)
        scatter(d)
        second_copy(d, gs).start()

    loop(1, n_gs, send_second)
    scatter(gs)
    back_in[gs] = back_out[gs]
    placed[...] = jnp.zeros_like(placed)

    def put_back(s):
        placed[...] += dot_t(stack(back_in[s], 3), pick_of(send, s, shard))

    put_back(gs)

    def put_next(k):
        s = lax.rem(gs + n_gs - k, n_gs)
        second_copy(gs, s).wait_recv()
        put_back(s)

    loop(1, n_gs, put_next)
    whole = fold(placed[...], 3)
    for c in range(chunks):
        views_out[view, 0:9, c, :] = whole[0:9, c * LANES : (c + 1) * LANES]
    first_row = lax.broadcasted_iota(jnp.int32, (chunks, LANES), 0) == 0
    views_out[view, 9] = jnp.where(first_row, cam_x, cam_y)

    def third_copy(to, of):
        return pltpu.make_async_remote_copy(
            src_ref=views_out.at[of],
            dst_ref=views_out.at[of],
            send_sem=send_three.at[to],
            recv_sem=recv_three.at[of],
            device_id=(gs, to),
            device_id_type=MESH,
        )

    def send_third(k):
        third_copy(lax.rem(view + k, n_view), view).start()

    def wait_third(k):
        third_copy(view, lax.rem(view + n_view - k, n_view)).wait_recv()

    loop(1, n_view, send_third)
    loop(1, n_view, wait_third)

    def done_first(k):
        first_copy(lax.rem(gs + k, n_gs), gs).wait_send()
        second_copy(lax.rem(gs + k, n_gs), gs).wait_send()

    def done_third(k):
        third_copy(lax.rem(view + k, n_view), view).wait_send()

    loop(1, n_gs, done_first)
    loop(1, n_view, done_third)


def pull_kernel(
    n_view,
    pic,
    views,
    par,
    opacity,
    pic_out,
    means_out,
    quats_out,
    scales_out,
    opacity_out,
    sh_out,
    g_par,
    g_means,
    g_quats,
    g_scales,
    g_opacity,
    g_sh,
    store_sems,
):
    chunks = par.shape[0]
    pic_copy = pltpu.make_async_copy(pic, pic_out, store_sems.at[0])
    pic_copy.start()
    cams = [(views[v, 9, 0:1, 0:1], views[v, 9, 1:2, 0:1]) for v in range(n_view)]
    _, pull = jax.vjp(lambda *args: project(*args, cams, 0.0, 0.0), *params(par, opacity))
    grads = pull([[views[v, i] for i in range(9)] for v in range(n_view)])
    for i in range(3):
        g_par[:, 48 + i, :] = grads[0][i]
        g_par[:, 64 + i, :] = grads[2][i]
    for i in range(4):
        g_par[:, 56 + i, :] = grads[1][i]
    for i in range(48):
        g_par[:, i, :] = grads[4][i]
    g_opacity[...] = grads[3]
    for c in range(chunks):
        cols = slice(c * LANES, (c + 1) * LANES)
        g_sh[:, cols] = g_par[c, 0:48, :]
        g_means[:, cols] = g_par[c, 48:51, :]
        g_quats[:, cols] = g_par[c, 56:60, :]
        g_scales[:, cols] = g_par[c, 64:67, :]
    stores = [
        pltpu.make_async_copy(src, dst, store_sems.at[k + 1])
        for k, (src, dst) in enumerate(
            [
                (g_sh, sh_out),
                (g_means, means_out),
                (g_quats, quats_out),
                (g_scales, scales_out),
                (g_opacity, opacity_out),
            ]
        )
    ]
    for store in stores:
        store.start()
    pic_copy.wait()
    for store in stores:
        store.wait()


def shards(
    means, quats, log_scales, opacity, sh_coeffs, cameras, targets, send_rows, tile_lists, list_lengths
):
    n_gs = lax.axis_size("gs")
    n_view = lax.axis_size("view")
    shard = means.shape[1]
    chunks = shard // LANES
    cap = send_rows.shape[2]
    tiles, list_size = tile_lists.shape[2:]
    width = tiles * TILE
    n_chunk = TILE // 2
    wide = 2 * width
    opacity = opacity.reshape(chunks, LANES)
    args = (
        means,
        quats,
        log_scales,
        opacity,
        sh_coeffs,
        cameras,
        targets,
        send_rows,
        tile_lists,
        list_lengths,
    )
    shape = jax.ShapeDtypeStruct
    dma = pltpu.SemaphoreType.DMA
    vmem = pl.BlockSpec(memory_space=VMEM)
    hbm = pl.BlockSpec(memory_space=pltpu.HBM)
    mids = pl.pallas_call(
        lambda *refs: train_kernel(n_gs, n_view, *refs),
        out_shape=(
            shape(targets.shape, f32),
            shape((n_view, 10, chunks, LANES), f32),
            shape((chunks, 72, LANES), f32),
            shape((chunks, LANES), f32),
        ),
        in_specs=[hbm] * len(args),
        out_specs=(vmem,) * 4,
        scratch_shapes=[
            VMEM(send_rows.shape, jnp.int32),
            VMEM(means.shape, f32),
            VMEM(quats.shape, f32),
            VMEM(log_scales.shape, f32),
            VMEM(sh_coeffs.shape, f32),
            VMEM(cameras.shape, f32),
            VMEM(targets.shape, f32),
            VMEM((tiles, list_size), jnp.int32),
            VMEM((1, tiles), jnp.int32),
            VMEM((chunks, ROWS_MSG, LANES), f32),
            VMEM((n_gs, ROWS_MSG, cap), f32),
            VMEM((n_gs, ROWS_MSG, cap), f32),
            VMEM((tiles, ROWS_MSG, list_size), f32),
            VMEM((n_chunk, list_size, wide), f32),
            VMEM((n_chunk, list_size, wide), f32),
            VMEM((3, TILE, width), f32),
            VMEM((2, 3, TILE, width), f32),
            VMEM((2, 3, TILE, width), f32),
            VMEM((tiles, ROWS_MSG, list_size), f32),
            VMEM((n_gs, ROWS_MSG, cap), f32),
            VMEM((n_gs, ROWS_MSG, cap), f32),
            VMEM((3 * ROWS_MSG, shard), f32),
            dma((10,)),
            dma((n_gs,)),
            dma((n_gs,)),
            dma((2,)),
            dma((2,)),
            dma((2,)),
            dma((2,)),
            dma((n_gs,)),
            dma((n_gs,)),
            dma((n_view,)),
            dma((n_view,)),
        ],
        compiler_params=pltpu.CompilerParams(
            collective_id=0, has_side_effects=True, vmem_limit_bytes=48 * 1024 * 1024
        ),
    )(*[pltpu.with_memory_space_constraint(x, pltpu.HBM) for x in args])
    outs = pl.pallas_call(
        lambda *refs: pull_kernel(n_view, *refs),
        out_shape=(
            shape(targets.shape, f32),
            shape(means.shape, f32),
            shape(quats.shape, f32),
            shape(log_scales.shape, f32),
            shape((chunks, LANES), f32),
            shape(sh_coeffs.shape, f32),
        ),
        in_specs=[vmem] * 4,
        out_specs=(hbm,) * 6,
        scratch_shapes=[
            VMEM((chunks, 72, LANES), f32),
            VMEM(means.shape, f32),
            VMEM(quats.shape, f32),
            VMEM(log_scales.shape, f32),
            VMEM((chunks, LANES), f32),
            VMEM(sh_coeffs.shape, f32),
            dma((6,)),
        ],
        compiler_params=pltpu.CompilerParams(vmem_limit_bytes=48 * 1024 * 1024),
    )(*mids)
    return (*outs[:4], outs[4].reshape(shard), outs[5])


def solution(mesh):
    return jax.shard_map(
        shards,
        mesh=mesh,
        in_specs=(
            P(None, "gs"),
            P(None, "gs"),
            P(None, "gs"),
            P("gs"),
            P(None, "gs"),
            P("view", None),
            P("view", None, "gs", None),
            P("gs", None, None),
            P("view", "gs", None, None),
            P("view", "gs", None),
        ),
        out_specs=(
            P("view", None, "gs", None),
            P(None, "gs"),
            P(None, "gs"),
            P(None, "gs"),
            P("gs"),
            P(None, "gs"),
        ),
        check_vma=False,
    )
```

profile of v0, /device:TPU:1, one launch (start us, length us, event | category | flops | bytes accessed | tf_op | source)
XLA Modules:
  0.0 33.8 jit_solution(16128575225347406125)
XLA Ops:
  0.6 30.0 %shard_map.145 = (f32[1,3,16,128]{3,2,1,0:T(8,128)S(1)}, f32[4,10,8,128]{3,2,1,0:T(8,128)S(1)}, f32[8,72,128]{2,1,0:T(8,128)S(1)}, f32[8,128]{1,0:T(8,128)S(1)}) custom-call(f32[3,1024]{1,0:T(4,128)} %refs_0_.1, f32[4,1024]{1,0:T(4,128)} %refs_1_.1, f32[3,1024]{1,0:T(4,128)} %refs_2_.1, f32[8,128]{1,0:T(8,128)} %bitcast.2, f32[48,1024]{1,0:T(8,128)} %refs_4_.1, ...), custom_call_target="tpu_custom_call" | custom-call | tf_op jit(solution)/shard_map/pallas_call | solution.py:725
  30.6 3.2 %shard_map.146 = (f32[1,3,16,128]{3,2,1,0:T(8,128)}, f32[3,1024]{1,0:T(4,128)}, f32[4,1024]{1,0:T(4,128)}, f32[3,1024]{1,0:T(4,128)}, f32[8,128]{1,0:T(8,128)}, /*index=5*/f32[48,1024]{1,0:T(8,128)}) custom-call(f32[1,3,16,128]{3,2,1,0:T(8,128)S(1)} %get-tuple-element.16.refs_0_, f32[4,10,8,128]{3,2,1,0:T(8,128)S(1)} %get-tuple-element.17.refs_1_, ...), custom_call_target="tpu_custom_call" | custom-call | tf_op jit(solution)/shard_map/pallas_call | solution.py:774
where the time goes:
time: 34.2 us; the launch traced here: 33.8 us
  Pallas kernels  33.2 us (97%)
  between operations  0.64 us (2%)
    pallas_call x1, Pallas kernels, shards(): pl.pallas_call(lambda *refs: train_kernel(n_gs, n_view, *refs), out_shape...  30 us
    pallas_call x1, Pallas kernels, shards(): pl.pallas_call(lambda *refs: pull_kernel(n_view, *refs), out_shape=(shape...  3.23 us

commit v1 on v0

--- a/solution.py
+++ b/solution.py
@@ -2,6 +2,8 @@
 
 import jax
 import jax.numpy as jnp
+import ml_dtypes
+import numpy as np
 from jax import lax
 from jax.experimental import pallas as pl
 from jax.experimental.pallas import tpu as pltpu
@@ -213,7 +215,716 @@
     return jnp.where(local_row == send[0, pl.ds(d, 1), :], 1.0, 0.0).astype(bf16)
 
 
-def train_kernel(
+def split_taps():
+    high = [float(np.asarray(tap, ml_dtypes.bfloat16)) for tap in window_taps()]
+    return high, [float(tap) - top for tap, top in zip(window_taps(), high)]
+
+
+def band_split(out_count, in_rows, offset, axis):
+    high, low = split_taps()
+    count = len(in_rows)
+    shape = (out_count, 3 * count) if axis == 1 else (3 * count, out_count)
+    inner = lax.broadcasted_iota(jnp.int32, shape, axis)
+    part = inner // count
+    place = lax.rem(inner, count)
+    start = in_rows[0]
+    jump = [k for k in range(1, count) if in_rows[k] != in_rows[k - 1] + 1]
+    row = place + start
+    for k in jump:
+        row = row + jnp.where(place >= k, in_rows[k] - in_rows[k - 1] - 1, 0)
+    gap = jnp.abs(row - lax.broadcasted_iota(jnp.int32, shape, 1 - axis) - offset)
+    matrix = jnp.zeros(shape, f32)
+    for far in range(RADIUS + 1):
+        tap = jnp.where(part == 2, low[RADIUS + far], high[RADIUS + far])
+        matrix = jnp.where(gap == far, tap, matrix)
+    return matrix.astype(bf16)
+
+
+def stack_mixed(x, axis):
+    high, low = pieces(x, 2)
+    return jnp.concatenate([high, low, high], axis=axis).astype(bf16)
+
+
+def side_by_side(x, count):
+    size = x.shape[1] // count
+    return jnp.concatenate([x[:, i * size : (i + 1) * size] for i in range(count)], axis=0)
+
+
+def pad_rows(x):
+    return jnp.concatenate([x, jnp.zeros((ROWS_MSG - x.shape[0], x.shape[1]), f32)], axis=0)
+
+
+def flip(index, bits):
+    bit = 1
+    while bit <= bits:
+        if bits & bit:
+            index = index + bit * (1 - 2 * lax.rem(lax.div(index, bit), 2))
+        bit *= 2
+    return index
+
+
+def spread_of(quats, log_scales):
+    inv_norm = 1.0 / jnp.sqrt(
+        quats[0] * quats[0] + quats[1] * quats[1] + quats[2] * quats[2] + quats[3] * quats[3]
+    )
+    w, x, y, z = [quat * inv_norm for quat in quats]
+    rotation = [
+        [1.0 - 2.0 * (y * y + z * z), 2.0 * (x * y - w * z), 2.0 * (x * z + w * y)],
+        [2.0 * (x * y + w * z), 1.0 - 2.0 * (x * x + z * z), 2.0 * (y * z - w * x)],
+        [2.0 * (x * z - w * y), 2.0 * (y * z + w * x), 1.0 - 2.0 * (x * x + y * y)],
+    ]
+    scales = [jnp.exp(log_scale) for log_scale in log_scales]
+    return [[rotation[i][j] * scales[j] for j in range(3)] for i in range(3)]
+
+
+def colours_of(coeffs, rel_x, rel_y, depth_z):
+    inv_dist = 1.0 / jnp.sqrt(rel_x * rel_x + rel_y * rel_y + depth_z * depth_z)
+    basis = sh_basis(rel_x * inv_dist, rel_y * inv_dist, depth_z * inv_dist)
+    out = []
+    for channel in range(3):
+        total = sh_c0 * coeffs[channel * SH] + 0.5
+        for k in range(1, SH):
+            total = total + coeffs[channel * SH + k] * basis[k]
+        out.append(total)
+    return out, basis
+
+
+N_KEPT = 45
+
+
+def keep_view(kept, coeffs, spread, means, inv_depth, jac_diag, cam_x, cam_y):
+    rel_x = means[0] - cam_x
+    rel_y = means[1] - cam_y
+    ratio_u = jac_diag * rel_x
+    ratio_v = jac_diag * rel_y
+    jac_u = -ratio_u * inv_depth
+    jac_v = -ratio_v * inv_depth
+    top = [jac_diag * spread[0][j] + jac_u * spread[2][j] for j in range(3)]
+    low = [jac_diag * spread[1][j] + jac_v * spread[2][j] for j in range(3)]
+    cov_a = top[0] * top[0] + top[1] * top[1] + top[2] * top[2] + cov_blur
+    cov_b = top[0] * low[0] + top[1] * low[1] + top[2] * low[2]
+    cov_c = low[0] * low[0] + low[1] * low[1] + low[2] * low[2] + cov_blur
+    inv_det = 1.0 / (cov_a * cov_c - cov_b * cov_b)
+    raw, pull, basis = jax.vjp(
+        lambda x, y, z: colours_of(coeffs, x, y, z), rel_x, rel_y, means[2], has_aux=True
+    )
+    out = [rel_x, rel_y, ratio_u, ratio_v, jac_u, jac_v] + top + low
+    out += [cov_c * inv_det, -cov_b * inv_det, cov_a * inv_det]
+    zero = jnp.zeros_like(rel_x)
+    one = jnp.ones_like(rel_x)
+    for channel in range(3):
+        out += pull([one if i == channel else zero for i in range(3)])
+    out += [jnp.where(x > 0.0, 1.0, jnp.where(x == 0.0, 0.5, 0.0)) for x in raw]
+    out += basis[1:]
+    for i, x in enumerate(out):
+        kept[i] = x
+
+
+def pull_view(kept, cots, inv_depth, jac_diag, spread):
+    rel_x, rel_y, ratio_u, ratio_v, jac_u, jac_v = [kept[i] for i in range(6)]
+    top = [kept[6 + j] for j in range(3)]
+    low = [kept[9 + j] for j in range(3)]
+    k0, k1, k2 = [kept[12 + i] for i in range(3)]
+    g0, g1, g2 = cots[2], cots[3], cots[4]
+    cov_a = -(k0 * k0 * g0 + k0 * k1 * g1 + k1 * k1 * g2)
+    cov_b = -2.0 * (k0 * k1 * g0 + k1 * k2 * g2) - (k0 * k2 + k1 * k1) * g1
+    cov_c = -(k1 * k1 * g0 + k1 * k2 * g1 + k2 * k2 * g2)
+    d_top = [2.0 * cov_a * top[j] + cov_b * low[j] for j in range(3)]
+    d_low = [2.0 * cov_c * low[j] + cov_b * top[j] for j in range(3)]
+    d_base = [jac_u * d_top[j] + jac_v * d_low[j] for j in range(3)]
+    d_jac_u = d_top[0] * spread[2][0] + d_top[1] * spread[2][1] + d_top[2] * spread[2][2]
+    d_jac_v = d_low[0] * spread[2][0] + d_low[1] * spread[2][1] + d_low[2] * spread[2][2]
+    d_ratio_u = cots[0] - inv_depth * d_jac_u
+    d_ratio_v = cots[1] - inv_depth * d_jac_v
+    shades = [cots[6 + c] * kept[24 + c] for c in range(3)]
+    turn = [
+        shades[0] * kept[15 + i] + shades[1] * kept[18 + i] + shades[2] * kept[21 + i]
+        for i in range(3)
+    ]
+    d_x = jac_diag * d_ratio_u + turn[0]
+    d_y = jac_diag * d_ratio_v + turn[1]
+    d_diag = rel_x * d_ratio_u + rel_y * d_ratio_v
+    d_inv = -(ratio_u * d_jac_u + ratio_v * d_jac_v)
+    return d_top + d_low + d_base + [d_x, d_y, turn[2], d_diag, d_inv, cots[5]], shades
+
+
+def near_kernel(
+    n_gs,
+    n_view,
+    means_in,
+    quats_in,
+    scales_in,
+    opacity_in,
+    sh_in,
+    camera_in,
+    targets_in,
+    send_in,
+    lists_in,
+    lens_in,
+    pic_out,
+    means_out,
+    quats_out,
+    scales_out,
+    opacity_out,
+    sh_out,
+    par,
+    opacity,
+    send,
+    means,
+    quats,
+    scales,
+    sh,
+    camera,
+    targets,
+    lists,
+    lens,
+    cams,
+    row_buf,
+    msg_out,
+    msg_in,
+    slot_mask,
+    slot_mask_t,
+    row_mask,
+    bases,
+    tile_buf,
+    ratio_buf,
+    weight_buf,
+    share_buf,
+    split_buf,
+    pic,
+    halo,
+    t_halo,
+    cot,
+    back_out,
+    back_in,
+    placed,
+    kept,
+    cot_views,
+    g_sum,
+    g_par,
+    load_sems,
+    send_cam,
+    recv_cam,
+    send_one,
+    recv_one,
+    send_halo,
+    recv_halo,
+    send_tgt,
+    recv_tgt,
+    send_two,
+    recv_two,
+    send_three,
+    recv_three,
+):
+    loads = [
+        pltpu.make_async_copy(src, dst, load_sems.at[k])
+        for k, (src, dst) in enumerate(
+            [
+                (sh_in, sh),
+                (means_in, means),
+                (quats_in, quats),
+                (scales_in, scales),
+                (opacity_in, opacity),
+                (camera_in, camera),
+                (send_in, send),
+                (lists_in.at[0, 0], lists),
+                (lens_in.at[0], lens),
+                (targets_in, targets),
+            ]
+        )
+    ]
+    for load in loads:
+        load.start()
+    gs = lax.axis_index("gs")
+    view = lax.axis_index("view")
+    shard = means.shape[1]
+    chunks = shard // LANES
+    cap = send.shape[2]
+    tiles, list_size = lists.shape
+    groups = n_view // 2
+    core = lax.rem(view, 2)
+    group = lax.div(view, 2)
+    has_up = gs > 0
+    has_down = gs < n_gs - 1
+    near = range(1, n_gs)
+    far = range(n_gs - 1, 0, -1)
+
+    def cousin(j):
+        return lax.rem(view + 2 * j, n_view)
+
+    barrier = pltpu.get_barrier_semaphore()
+
+    def greet(strip, cam):
+        pl.semaphore_signal(barrier, inc=1, device_id=(strip, cam), device_id_type=MESH)
+
+    for k in near:
+        greet(flip(gs, k), view)
+    for j in range(1, groups):
+        for k in range(n_gs):
+            greet(flip(gs, k), cousin(j))
+    for j in range(groups):
+        greet(gs, flip(cousin(j), 1))
+    greeted = n_gs - 1 + (groups - 1) * n_gs + groups
+
+    for load in loads[:7]:
+        load.wait()
+
+    for c in range(chunks):
+        cols = slice(c * LANES, (c + 1) * LANES)
+        par[c, 0:48, :] = sh[:, cols]
+        par[c, 48:51, :] = means[:, cols]
+        par[c, 56:60, :] = quats[:, cols]
+        par[c, 64:67, :] = scales[:, cols]
+
+    centre_x = 0.5 * tiles * TILE
+    centre_y = 0.5 * n_gs * TILE
+    cam_x = camera[0:1, 0:1]
+    cam_y = camera[0:1, 1:2]
+    rows = project(*params(par, opacity), [(cam_x, cam_y)], centre_x, centre_y)[0]
+    row_buf[...] = jnp.zeros_like(row_buf)
+    for i in range(9):
+        row_buf[:, i, :] = rows[i]
+    table = stack(jnp.concatenate([row_buf[c] for c in range(chunks)], axis=1), 3)
+
+    def fill(d):
+        msg_out[d] = fold(dot(table, pick_of(send, d, shard)), 3)[0:9]
+
+    def first_copy(d, s):
+        return pltpu.make_async_remote_copy(
+            src_ref=msg_out.at[d],
+            dst_ref=msg_in.at[s],
+            send_sem=send_one.at[d],
+            recv_sem=recv_one.at[s],
+            device_id=(d, view),
+            device_id_type=MESH,
+        )
+
+    pl.semaphore_wait(barrier, greeted)
+
+    for k in far:
+        fill(flip(gs, k))
+        first_copy(flip(gs, k), gs).start()
+    fill(gs)
+    msg_in[gs] = msg_out[gs]
+
+    def cam_copy(to, of):
+        return pltpu.make_async_remote_copy(
+            src_ref=cams.at[of],
+            dst_ref=cams.at[of],
+            send_sem=send_cam.at[to],
+            recv_sem=recv_cam.at[of],
+            device_id=(gs, to),
+            device_id_type=MESH,
+        )
+
+    lane_one = lax.broadcasted_iota(jnp.int32, (1, LANES), 1)
+    cams[view] = jnp.where(lane_one == 0, cam_x, cam_y)
+    for k in range(1, n_view):
+        cam_copy(lax.rem(view + k, n_view), view).start()
+
+    def halo_copy(src, dst, sends, recvs, side):
+        other = gs + 1 if side == 0 else gs - 1
+        return pltpu.make_async_remote_copy(
+            src_ref=src,
+            dst_ref=dst.at[side],
+            send_sem=sends.at[side],
+            recv_sem=recvs.at[side],
+            device_id=(other, view),
+            device_id_type=MESH,
+        )
+
+    def exchange(src, dst, sends, recvs, start, ends=(False, True)):
+        def act(copy, recv):
+            if start:
+                copy.start()
+            elif recv:
+                copy.wait_recv()
+            else:
+                copy.wait_send()
+
+        for recv in ends:
+            if start and recv:
+                continue
+
+            @pl.when(has_down)
+            def _():
+                act(halo_copy(src, dst, sends, recvs, 1 if recv else 0), recv)
+
+            @pl.when(has_up)
+            def _():
+                act(halo_copy(src, dst, sends, recvs, 0 if recv else 1), recv)
+
+    for load in loads[7:]:
+        load.wait()
+    exchange(targets.at[0], t_halo, send_tgt, recv_tgt, True)
+
+    @pl.when(jnp.logical_not(has_up))
+    def _():
+        halo[0] = jnp.zeros_like(halo[0])
+        t_halo[0] = jnp.zeros_like(t_halo[0])
+
+    @pl.when(jnp.logical_not(has_down))
+    def _():
+        halo[1] = jnp.zeros_like(halo[1])
+        t_halo[1] = jnp.zeros_like(t_halo[1])
+
+    n_chunk, _, wide = weight_buf.shape
+    width = tiles * TILE
+    per = wide // width
+    slot_row = lax.broadcasted_iota(jnp.int32, (cap, list_size), 0)
+    for k in range(n_gs):
+        here = slot_row + flip(gs, k) * cap
+        for t in range(tiles):
+            slot_mask[k, :, t * list_size : (t + 1) * list_size] = jnp.where(
+                here == lists[t : t + 1, :], 1.0, 0.0
+            ).astype(bf16)
+    lists_t = jnp.transpose(lists[...].astype(f32))
+    slot_lane = lax.broadcasted_iota(jnp.int32, (list_size, cap), 1)
+    for t in range(tiles):
+        listed = jnp.broadcast_to(lists_t[:, t : t + 1], (list_size, cap))
+        for k in range(n_gs):
+            here = (slot_lane + flip(gs, k) * cap).astype(f32)
+            slot_mask_t[k, t * list_size : (t + 1) * list_size, :] = jnp.where(
+                here == listed, 1.0, 0.0
+            ).astype(bf16)
+
+    lane = lax.broadcasted_iota(jnp.int32, (tiles, wide), 1)
+    in_tile = lax.rem(lane, width) // TILE == lax.broadcasted_iota(jnp.int32, (tiles, wide), 0)
+    off_q = (lax.rem(lane, TILE) - TILE // 2).astype(f32)
+    half_r = (lane // width).astype(f32)
+    for i in range(n_chunk):
+        off_r = half_r + float(i * per - TILE // 2)
+        out = [jnp.ones_like(off_q), off_q, off_r, off_q * off_q, off_q * off_r, off_r * off_r]
+        bases[i] = jnp.concatenate([jnp.where(in_tile, x, 0.0) for x in out], axis=0).astype(bf16)
+    shape = (list_size, 2 * list_size)
+    list_row = lax.broadcasted_iota(jnp.int32, shape, 0)
+    list_col = lax.rem(lax.broadcasted_iota(jnp.int32, shape, 1), list_size)
+    prefix = jnp.where(list_col < list_row, 1.0, 0.0).astype(bf16)
+    suffix = jnp.where(list_col > list_row, 1.0, 0.0).astype(bf16)
+    for t in range(tiles):
+        tile_buf[t] = jnp.zeros((ROWS_MSG, list_size), f32)
+
+    def gather(k, s):
+        got = fold(dot(stack(pad_rows(msg_in[s]), 3), slot_mask[k]), 3)
+        for t in range(tiles):
+            tile_buf[t] += got[:, t * list_size : (t + 1) * list_size]
+
+    gather(0, gs)
+    for k in near:
+        s = flip(gs, k)
+        first_copy(gs, s).wait_recv()
+        gather(k, s)
+
+    diagonal = lax.broadcasted_iota(jnp.int32, (tiles, tiles), 0) == lax.broadcasted_iota(
+        jnp.int32, (tiles, tiles), 1
+    )
+    used = jnp.sum(jnp.where(diagonal, lens[...].astype(f32), 0.0), axis=1, keepdims=True)
+    entry = lax.broadcasted_iota(jnp.int32, (tiles, list_size), 1)
+    live = entry.astype(f32) < used
+    mid_q = (lax.broadcasted_iota(jnp.int32, (tiles, list_size), 0) * TILE + TILE // 2).astype(f32)
+    mid_r = (gs * TILE + TILE // 2).astype(f32)
+    off_u = tile_buf[:, 0, :] - mid_q
+    off_w = tile_buf[:, 1, :] - mid_r
+    k0 = tile_buf[:, 2, :]
+    k1 = tile_buf[:, 3, :]
+    k2 = tile_buf[:, 4, :]
+    lin_u = k0 * off_u + k1 * off_w
+    lin_w = k2 * off_w + k1 * off_u
+    terms = [
+        jnp.where(live, tile_buf[:, 5, :] - 0.5 * (off_u * lin_u + off_w * lin_w), -10000.0),
+        jnp.where(live, lin_u, 0.0),
+        jnp.where(live, lin_w, 0.0),
+        jnp.where(live, -0.5 * k0, 0.0),
+        jnp.where(live, -k1, 0.0),
+        jnp.where(live, -0.5 * k2, 0.0),
+    ]
+    term_t = jnp.transpose(jnp.concatenate(pieces(jnp.concatenate(terms, axis=0), 3), axis=0))
+    term_t = term_t.astype(bf16)
+    colour = jnp.concatenate([tile_buf[:, 6 + c, :] for c in range(3)], axis=0)
+    col_hi, col_lo = pieces(colour, 2)
+    col_two = jnp.concatenate([col_hi, col_lo], axis=0)
+    col_wide = jnp.concatenate([col_two, col_two], axis=1).astype(bf16)
+    col_t = jnp.transpose(jnp.concatenate([col_hi, col_lo, col_hi], axis=0)).astype(bf16)
+
+    for i in range(n_chunk):
+        base = bases[i]
+        ratio_buf[i] = jnp.exp(dot(term_t, jnp.concatenate([base, base, base], axis=0)))
+    for i in range(n_chunk):
+        alpha = ratio_buf[i]
+        weight = alpha * jnp.exp(dot(prefix, stack(jnp.log(1.0 - alpha), 2)))
+        weight_buf[i] = weight
+        split_buf[i] = stack(weight, 2)
+    for i in range(n_chunk):
+        drawn = fold(dot(col_wide, split_buf[i]), 2)
+        for c in range(3):
+            mine = jnp.where(in_tile, drawn[c * tiles : (c + 1) * tiles], 0.0)
+            line = jnp.sum(mine, axis=0, keepdims=True)
+            for half in range(per):
+                row = i * per + half
+                pic[c, row : row + 1, :] = line[:, half * width : (half + 1) * width]
+
+    exchange(pic, halo, send_halo, recv_halo, True)
+    pic_out[0] = pic[...]
+    exchange(targets.at[0], t_halo, send_tgt, recv_tgt, False)
+    tall = 2 * TILE
+    across = band_split(width, list(range(width)), 0, 0)
+    tgts = [
+        jnp.concatenate([t_halo[0, c], targets[0, c], t_halo[1, c]], axis=0) for c in range(3)
+    ]
+    planes = []
+    for c in range(3):
+        planes += [tgts[c], tgts[c] * tgts[c]]
+    rows_all = list(range(3 * TILE))
+    band_all = band_split(tall, rows_all, TILE // 2, 1)
+    down = dot(band_all, stack_mixed(jnp.concatenate(planes, axis=1), 0))
+    blur_tgt = dot(stack_mixed(side_by_side(down, 6), 1), across)
+    own = []
+    for c in range(3):
+        img = pic[c]
+        own += [img, img * img, img * targets[0, c]]
+    band_own = band_split(tall, rows_all[TILE : 2 * TILE], TILE // 2, 1)
+    down_own = dot(band_own, stack_mixed(jnp.concatenate(own, axis=1), 0))
+    band_far = band_split(tall, rows_all[:TILE] + rows_all[2 * TILE :], TILE // 2, 1)
+    band_back = band_split(TILE, list(range(tall)), TILE // 2, 1)
+    directs = []
+    for c in range(3):
+        res = pic[c] - targets[0, c]
+        directs.append(
+            (1.0 - ssim_weight) / (TILE * TILE) * res / jnp.sqrt(res * res + charb_eps)
+        )
+    for i in range(n_chunk):
+        alpha = ratio_buf[i]
+        ratio_buf[i] = alpha / (1.0 - alpha)
+    exchange(pic, halo, send_halo, recv_halo, False)
+
+    beyond = []
+    for c in range(3):
+        img = jnp.concatenate([halo[0, c], halo[1, c]], axis=0)
+        tgt = jnp.concatenate([t_halo[0, c], t_halo[1, c]], axis=0)
+        beyond += [img, img * img, img * tgt]
+    down = down_own + dot(band_far, stack_mixed(jnp.concatenate(beyond, axis=1), 0))
+    blurred = dot(stack_mixed(side_by_side(down, 9), 1), across)
+    at_row = lax.broadcasted_iota(jnp.int32, (tall, width), 0) + gs * TILE - TILE // 2
+    inside = jnp.logical_and(at_row >= 0, at_row < n_gs * TILE)
+    scale = -ssim_weight / (TILE * TILE)
+    cots = []
+    for c in range(3):
+        mean_x, raw_xx, raw_xy = [
+            blurred[(3 * c + i) * tall : (3 * c + i + 1) * tall] for i in range(3)
+        ]
+        mean_y, raw_yy = [
+            blur_tgt[(2 * c + i) * tall : (2 * c + i + 1) * tall] for i in range(2)
+        ]
+        top_a = 2.0 * mean_x * mean_y + ssim_one
+        top_b = 2.0 * (raw_xy - mean_x * mean_y) + ssim_two
+        low_c = mean_x * mean_x + mean_y * mean_y + ssim_one
+        low_d = (raw_xx - mean_x * mean_x) + (raw_yy - mean_y * mean_y) + ssim_two
+        inv_cd = 1.0 / (low_c * low_d)
+        inv_dd = inv_cd * low_c
+        ssim = top_a * top_b * inv_cd
+        d_mean = 2.0 * mean_y * (top_b - top_a) * inv_cd - 2.0 * mean_x * ssim * (
+            inv_cd * low_d - inv_dd
+        )
+        d_xx = -ssim * inv_dd
+        d_xy = 2.0 * top_a * inv_cd
+        cots += [jnp.where(inside, scale * part, 0.0) for part in (d_mean, d_xx, d_xy)]
+    spread = dot(band_back, stack_mixed(jnp.concatenate(cots, axis=1), 0))
+    spread = dot(stack_mixed(side_by_side(spread, 9), 1), across)
+    grad_rows = []
+    for c in range(3):
+        s_mean, s_xx, s_xy = [spread[(3 * c + i) * TILE : (3 * c + i + 1) * TILE] for i in range(3)]
+        grad_rows.append(directs[c] + s_mean + 2.0 * pic[c] * s_xx + targets[0, c] * s_xy)
+
+    shades = []
+    for i in range(n_chunk):
+        parts = []
+        for c in range(3):
+            line = jnp.concatenate(
+                [grad_rows[c][i * per + half : i * per + half + 1] for half in range(per)], axis=1
+            )
+            parts.append(jnp.where(in_tile, line, 0.0))
+        hi, lo = pieces(jnp.concatenate(parts, axis=0), 2)
+        shades.append(jnp.concatenate([hi, lo], axis=0).astype(bf16))
+        shade = dot(col_t, jnp.concatenate([hi, hi, lo], axis=0).astype(bf16))
+        share_buf[i] = weight_buf[i] * shade
+    for i in range(n_chunk):
+        share = share_buf[i]
+        share_buf[i] = share - ratio_buf[i] * dot(suffix, stack(share, 2))
+    d_terms = jnp.zeros((6 * tiles, 2 * list_size), f32)
+    d_colour = jnp.zeros((6 * tiles, 2 * list_size), f32)
+    for i in range(n_chunk):
+        d_terms = d_terms + dot_t(bases[i], stack(share_buf[i], 2))
+        d_colour = d_colour + dot_t(shades[i], split_buf[i])
+    d_terms = d_terms[:, :list_size] + d_terms[:, list_size:]
+    d_colour = fold(d_colour[:, :list_size] + d_colour[:, list_size:], 2)
+
+    d0, d1, d2, d3, d4, d5 = [d_terms[k * tiles : (k + 1) * tiles] for k in range(6)]
+    e1 = d1 - off_u * d0
+    e2 = d2 - off_w * d0
+    cot[...] = jnp.zeros_like(cot)
+    cot[:, 0, :] = k0 * e1 + k1 * e2
+    cot[:, 1, :] = k2 * e2 + k1 * e1
+    cot[:, 2, :] = -0.5 * d3 + off_u * (d1 - 0.5 * off_u * d0)
+    cot[:, 3, :] = off_w * e1 + off_u * d2 - d4
+    cot[:, 4, :] = -0.5 * d5 + off_w * (d2 - 0.5 * off_w * d0)
+    cot[:, 5, :] = d0
+    for c in range(3):
+        cot[:, 6 + c, :] = d_colour[c * tiles : (c + 1) * tiles]
+    cots = jnp.concatenate([stack(cot[t], 2) for t in range(tiles)], axis=1)
+
+    def out_copy(j, d):
+        return pltpu.make_async_remote_copy(
+            src_ref=back_out.at[d],
+            dst_ref=back_in.at[group, gs],
+            send_sem=send_two.at[j, d],
+            recv_sem=recv_two.at[group, gs],
+            device_id=(d, cousin(j)),
+            device_id_type=MESH,
+        )
+
+    def in_copy(j, s):
+        of = lax.div(cousin(j), 2)
+        return pltpu.make_async_remote_copy(
+            src_ref=back_out.at[s],
+            dst_ref=back_in.at[of, s],
+            send_sem=send_two.at[j, s],
+            recv_sem=recv_two.at[of, s],
+            device_id=(s, cousin(j)),
+            device_id_type=MESH,
+        )
+
+    for k in list(far) + [0]:
+        d = flip(gs, k)
+        back_out[d] = fold(dot(cots, slot_mask_t[k]), 2)[0:9]
+        for j in range(groups):
+            if k or j:
+                out_copy(j, d).start()
+    back_in[group, gs] = back_out[gs]
+
+    send_t = jnp.transpose(send[0].astype(f32))
+    shard_lane = lax.broadcasted_iota(jnp.int32, (cap, shard), 1).astype(f32)
+    for s in range(n_gs):
+        row_mask[s] = jnp.where(shard_lane == send_t[:, s : s + 1], 1.0, 0.0).astype(bf16)
+    for k in range(1, n_view):
+        cam_copy(view, lax.rem(view + n_view - k, n_view)).wait_recv()
+    p_means, p_quats, p_scales, p_opacity, p_coeffs = params(par, opacity)
+    spread, pull_spread = jax.vjp(spread_of, p_quats, p_scales)
+    inv_depth = 1.0 / p_means[2]
+    jac_diag = focal_length * inv_depth
+    for h in range(2):
+        for j in range(groups):
+            of = 2 * j + (core if h == 0 else 1 - core)
+            at = cams[of]
+            keep_view(
+                kept.at[h, j], p_coeffs, spread, p_means, inv_depth, jac_diag, at[:, 0:1], at[:, 1:2]
+            )
+
+    placed[...] = jnp.zeros_like(placed)
+
+    def put_back(s):
+        both = [stack(pad_rows(back_in[j, s]), 2) for j in range(groups)]
+        placed[...] += dot(jnp.concatenate(both, axis=0), row_mask[s])
+
+    for k in range(n_gs):
+        s = flip(gs, k)
+        for j in range(groups):
+            if k or j:
+                in_copy(j, s).wait_recv()
+        put_back(s)
+    for j in range(groups):
+        mine = fold(placed[2 * ROWS_MSG * j : 2 * ROWS_MSG * (j + 1)], 2)
+        for c in range(chunks):
+            cot_views[core, j, :, c, :] = mine[0:9, c * LANES : (c + 1) * LANES]
+
+    def third_copy(of):
+        return pltpu.make_async_remote_copy(
+            src_ref=cot_views.at[of],
+            dst_ref=cot_views.at[of],
+            send_sem=send_three.at[0],
+            recv_sem=recv_three.at[0],
+            device_id=(gs, flip(view, 1)),
+            device_id_type=MESH,
+        )
+
+    third_copy(core).start()
+
+    def pull_half(h):
+        side = core if h == 0 else 1 - core
+        total = None
+        tints = []
+        for j in range(groups):
+            cots = [cot_views[side, j, i] for i in range(9)]
+            got, shades = pull_view(kept.at[h, j], cots, inv_depth, jac_diag, spread)
+            total = got if total is None else [a + b for a, b in zip(total, got)]
+            tints.append(shades)
+        for i in range(15):
+            if h == 0:
+                g_sum[i] = total[i]
+            else:
+                total[i] = total[i] + g_sum[i]
+        for k in range(SH):
+            for c in range(3):
+                part = None
+                for j in range(groups):
+                    term = tints[j][c] * (sh_c0 if k == 0 else kept[h, j, 26 + k])
+                    part = term if part is None else part + term
+                if h == 1:
+                    part = part + g_par[:, c * SH + k, :]
+                g_par[:, c * SH + k, :] = part
+        return total
+
+    pull_half(0)
+    third_copy(1 - core).wait_recv()
+    total = pull_half(1)
+    d_top, d_low, d_base = total[0:3], total[3:6], total[6:9]
+    d_x, d_y, d_z, d_diag, d_inv, d_log = total[9:15]
+    for j in range(3):
+        d_diag = d_diag + d_top[j] * spread[0][j] + d_low[j] * spread[1][j]
+    d_inv = d_inv + focal_length * d_diag
+    d_z = d_z - inv_depth * inv_depth * d_inv
+    d_quats, d_scales = pull_spread(
+        [[jac_diag * x for x in d_top], [jac_diag * x for x in d_low], list(d_base)]
+    )
+    decay = jnp.exp(-p_opacity)
+    opacity_out[...] = d_log * decay / (1.0 + decay)
+    for i, x in enumerate([d_x, d_y, d_z]):
+        g_par[:, 48 + i, :] = x
+    for i in range(4):
+        g_par[:, 56 + i, :] = d_quats[i]
+    for i in range(3):
+        g_par[:, 64 + i, :] = d_scales[i]
+    for c in range(chunks):
+        cols = slice(c * LANES, (c + 1) * LANES)
+        sh_out[:, cols] = g_par[c, 0:48, :]
+        means_out[:, cols] = g_par[c, 48:51, :]
+        quats_out[:, cols] = g_par[c, 56:60, :]
+        scales_out[:, cols] = g_par[c, 64:67, :]
+
+    for k in near:
+        first_copy(flip(gs, k), gs).wait_send()
+    for k in range(1, n_view):
+        cam_copy(lax.rem(view + k, n_view), view).wait_send()
+    for k in range(n_gs):
+        for j in range(groups):
+            if k or j:
+                out_copy(j, flip(gs, k)).wait_send()
+    third_copy(core).wait_send()
+
+
+def store_kernel(*refs):
+    count = len(refs) // 2
+    sources, places, sems = refs[:count], refs[count : 2 * count], refs[-1]
+    stores = [
+        pltpu.make_async_copy(src, dst, sems.at[k])
+        for k, (src, dst) in enumerate(zip(sources, places))
+    ]
+    for store in stores:
+        store.start()
+    for store in stores:
+        store.wait()
+
+
+def far_kernel(
     n_gs,
     n_view,
     means_in,
@@ -693,7 +1404,7 @@
         store.wait()
 
 
-def shards(
+def far_shards(
     means, quats, log_scales, opacity, sh_coeffs, cameras, targets, send_rows, tile_lists, list_lengths
 ):
     n_gs = lax.axis_size("gs")
@@ -723,7 +1434,7 @@
     vmem = pl.BlockSpec(memory_space=VMEM)
     hbm = pl.BlockSpec(memory_space=pltpu.HBM)
     mids = pl.pallas_call(
-        lambda *refs: train_kernel(n_gs, n_view, *refs),
+        lambda *refs: far_kernel(n_gs, n_view, *refs),
         out_shape=(
             shape(targets.shape, f32),
             shape((n_view, 10, chunks, LANES), f32),
@@ -797,6 +1508,116 @@
     return (*outs[:4], outs[4].reshape(shard), outs[5])
 
 
+def shards(
+    means, quats, log_scales, opacity, sh_coeffs, cameras, targets, send_rows, tile_lists, list_lengths
+):
+    n_gs = lax.axis_size("gs")
+    n_view = lax.axis_size("view")
+    shard = means.shape[1]
+    cap = send_rows.shape[2]
+    args = (
+        means,
+        quats,
+        log_scales,
+        opacity,
+        sh_coeffs,
+        cameras,
+        targets,
+        send_rows,
+        tile_lists,
+        list_lengths,
+    )
+    if n_gs not in (2, 4, 8) or cap % LANES or n_view % 2:
+        return far_shards(*args)
+    chunks = shard // LANES
+    tiles, list_size = tile_lists.shape[2:]
+    width = tiles * TILE
+    n_chunk = TILE // 2
+    wide = 2 * width
+    groups = n_view // 2
+    args = args[:3] + (opacity.reshape(chunks, LANES),) + args[4:]
+    shape = jax.ShapeDtypeStruct
+    dma = pltpu.SemaphoreType.DMA
+    vmem = pl.BlockSpec(memory_space=VMEM)
+    hbm = pl.BlockSpec(memory_space=pltpu.HBM)
+    out_shape = (
+        shape(targets.shape, f32),
+        shape(means.shape, f32),
+        shape(quats.shape, f32),
+        shape(log_scales.shape, f32),
+        shape((chunks, LANES), f32),
+        shape(sh_coeffs.shape, f32),
+    )
+    mids = pl.pallas_call(
+        lambda *refs: near_kernel(n_gs, n_view, *refs),
+        out_shape=out_shape,
+        in_specs=[hbm] * len(args),
+        out_specs=(vmem,) * 6,
+        scratch_shapes=[
+            VMEM((chunks, 72, LANES), f32),
+            VMEM((chunks, LANES), f32),
+            VMEM(send_rows.shape, jnp.int32),
+            VMEM(means.shape, f32),
+            VMEM(quats.shape, f32),
+            VMEM(log_scales.shape, f32),
+            VMEM(sh_coeffs.shape, f32),
+            VMEM(cameras.shape, f32),
+            VMEM(targets.shape, f32),
+            VMEM((tiles, list_size), jnp.int32),
+            VMEM((1, tiles), jnp.int32),
+            VMEM((n_view, 1, LANES), f32),
+            VMEM((chunks, ROWS_MSG, LANES), f32),
+            VMEM((n_gs, 9, cap), f32),
+            VMEM((n_gs, 9, cap), f32),
+            VMEM((n_gs, cap, tiles * list_size), bf16),
+            VMEM((n_gs, tiles * list_size, cap), bf16),
+            VMEM((n_gs, cap, shard), bf16),
+            VMEM((n_chunk, 6 * tiles, wide), bf16),
+            VMEM((tiles, ROWS_MSG, list_size), f32),
+            VMEM((n_chunk, list_size, wide), f32),
+            VMEM((n_chunk, list_size, wide), f32),
+            VMEM((n_chunk, list_size, wide), f32),
+            VMEM((n_chunk, 2 * list_size, wide), bf16),
+            VMEM((3, TILE, width), f32),
+            VMEM((2, 3, TILE, width), f32),
+            VMEM((2, 3, TILE, width), f32),
+            VMEM((tiles, ROWS_MSG, list_size), f32),
+            VMEM((n_gs, 9, cap), f32),
+            VMEM((groups, n_gs, 9, cap), f32),
+            VMEM((2 * ROWS_MSG * groups, shard), f32),
+            VMEM((2, groups, N_KEPT, chunks, LANES), f32),
+            VMEM((2, groups, 9, chunks, LANES), f32),
+            VMEM((15, chunks, LANES), f32),
+            VMEM((chunks, 72, LANES), f32),
+            dma((10,)),
+            dma((n_view,)),
+            dma((n_view,)),
+            dma((n_gs,)),
+            dma((n_gs,)),
+            dma((2,)),
+            dma((2,)),
+            dma((2,)),
+            dma((2,)),
+            dma((groups, n_gs)),
+            dma((groups, n_gs)),
+            dma((1,)),
+            dma((1,)),
+        ],
+        compiler_params=pltpu.CompilerParams(
+            collective_id=1, has_side_effects=True, vmem_limit_bytes=48 * 1024 * 1024
+        ),
+    )(*[pltpu.with_memory_space_constraint(x, pltpu.HBM) for x in args])
+    outs = pl.pallas_call(
+        store_kernel,
+        out_shape=out_shape,
+        in_specs=[vmem] * 6,
+        out_specs=(hbm,) * 6,
+        scratch_shapes=[dma((6,))],
+        compiler_params=pltpu.CompilerParams(vmem_limit_bytes=48 * 1024 * 1024),
+    )(*mids)
+    return (*outs[:4], outs[4].reshape(shard), outs[5])
+
+
 def solution(mesh):
     return jax.shard_map(
         shards,

time: 34.2 us -> 27.1 us (0.79)
  Pallas kernels: 33.2 us -> 26.3 us
    pallas_call x2, Pallas kernels: 33.2 us -> 26.3 us  [the longest x1 25.5 us: shards(): pl.pallas_call(lambda *refs: near_kernel(n_gs, n_view, *refs), out_shape=...]
where the time goes in v1:
time: 27.1 us; the launch traced here: 26.9 us
  Pallas kernels  26.3 us (97%)
  between operations  0.64 us (2%)
    pallas_call x1, Pallas kernels, shards(): pl.pallas_call(lambda *refs: near_kernel(n_gs, n_view, *refs), out_shape=...  25.5 us
    pallas_call x1, Pallas kernels, shards(): pl.pallas_call(store_kernel, out_shape=out_shape, in_specs=[vmem] * 6, ou...  0.76 us

profile of v1, /device:TPU:1, one launch (start us, length us, event | category | flops | bytes accessed | tf_op | source)
XLA Modules:
  0.0 26.9 jit_solution(1542452139007604789)
XLA Ops:
  0.6 25.5 %shard_map.145 = (f32[1,3,16,128]{3,2,1,0:T(8,128)S(1)}, f32[3,1024]{1,0:T(4,128)S(1)}, f32[4,1024]{1,0:T(4,128)S(1)}, f32[3,1024]{1,0:T(4,128)S(1)}, f32[8,128]{1,0:T(8,128)S(1)}, /*index=5*/f32[48,1024]{1,0:T(8,128)S(1)}) custom-call(f32[3,1024]{1,0:T(4,128)} %refs_0_.1, f32[4,1024]{1,0:T(4,128)} %refs_1_.1, f32[3,1024]{1,0:T(4,128)} %refs_2_.1, ...), custom_call_target="tpu_custom_call" | custom-call | tf_op jit(solution)/shard_map/pallas_call | solution.py:1551
  26.2 0.8 %shard_map.146 = (f32[1,3,16,128]{3,2,1,0:T(8,128)}, f32[3,1024]{1,0:T(4,128)}, f32[4,1024]{1,0:T(4,128)}, f32[3,1024]{1,0:T(4,128)}, f32[8,128]{1,0:T(8,128)}, /*index=5*/f32[48,1024]{1,0:T(8,128)}) custom-call(f32[1,3,16,128]{3,2,1,0:T(8,128)S(1)} %get-tuple-element.18.refs_0_, f32[3,1024]{1,0:T(4,128)S(1)} %get-tuple-element.19.refs_1_, ...), custom_call_target="tpu_custom_call" | custom-call | tf_op jit(solution)/shard_map/pallas_call | solution.py:1610

commit v2 on v1

--- a/solution.py
+++ b/solution.py
@@ -277,22 +277,58 @@
     return [[rotation[i][j] * scales[j] for j in range(3)] for i in range(3)]
 
 
-def colours_of(coeffs, rel_x, rel_y, depth_z):
-    inv_dist = 1.0 / jnp.sqrt(rel_x * rel_x + rel_y * rel_y + depth_z * depth_z)
-    basis = sh_basis(rel_x * inv_dist, rel_y * inv_dist, depth_z * inv_dist)
-    out = []
-    for channel in range(3):
-        total = sh_c0 * coeffs[channel * SH] + 0.5
-        for k in range(1, SH):
-            total = total + coeffs[channel * SH + k] * basis[k]
-        out.append(total)
-    return out, basis
-
-
-N_KEPT = 45
-
-
-def keep_view(kept, coeffs, spread, means, inv_depth, jac_diag, cam_x, cam_y):
+def basis_slopes(x, y, z):
+    xx, yy, zz = x * x, y * y, z * z
+    xy, yz, xz = x * y, y * z, x * z
+    gap = xx - yy
+    four = 4.0 * zz
+    return [
+        {
+            3: -sh_c1,
+            4: sh_c2[0] * y,
+            6: -2.0 * sh_c2[2] * x,
+            7: sh_c2[3] * z,
+            8: 2.0 * sh_c2[4] * x,
+            9: 6.0 * sh_c3[0] * xy,
+            10: sh_c3[1] * yz,
+            11: -2.0 * sh_c3[2] * xy,
+            12: -6.0 * sh_c3[3] * xz,
+            13: sh_c3[4] * (four - 3.0 * xx - yy),
+            14: 2.0 * sh_c3[5] * xz,
+            15: 3.0 * sh_c3[6] * gap,
+        },
+        {
+            1: -sh_c1,
+            4: sh_c2[0] * x,
+            5: sh_c2[1] * z,
+            6: -2.0 * sh_c2[2] * y,
+            8: -2.0 * sh_c2[4] * y,
+            9: 3.0 * sh_c3[0] * gap,
+            10: sh_c3[1] * xz,
+            11: sh_c3[2] * (four - xx - 3.0 * yy),
+            12: -6.0 * sh_c3[3] * yz,
+            13: -2.0 * sh_c3[4] * xy,
+            14: -2.0 * sh_c3[5] * yz,
+            15: -6.0 * sh_c3[6] * xy,
+        },
+        {
+            2: sh_c1,
+            5: sh_c2[1] * y,
+            6: 4.0 * sh_c2[2] * z,
+            7: sh_c2[3] * x,
+            10: sh_c3[1] * xy,
+            11: 8.0 * sh_c3[2] * yz,
+            12: sh_c3[3] * (6.0 * zz - 3.0 * xx - 3.0 * yy),
+            13: 8.0 * sh_c3[4] * xz,
+            14: sh_c3[5] * gap,
+        },
+    ]
+
+
+N_KEPT = 42
+
+
+def keep_view(kept, par, spread, means, inv_depth, jac_diag, cam_x, cam_y):
     rel_x = means[0] - cam_x
     rel_y = means[1] - cam_y
     ratio_u = jac_diag * rel_x
@@ -305,19 +341,30 @@
     cov_b = top[0] * low[0] + top[1] * low[1] + top[2] * low[2]
     cov_c = low[0] * low[0] + low[1] * low[1] + low[2] * low[2] + cov_blur
     inv_det = 1.0 / (cov_a * cov_c - cov_b * cov_b)
-    raw, pull, basis = jax.vjp(
-        lambda x, y, z: colours_of(coeffs, x, y, z), rel_x, rel_y, means[2], has_aux=True
-    )
     out = [rel_x, rel_y, ratio_u, ratio_v, jac_u, jac_v] + top + low
     out += [cov_c * inv_det, -cov_b * inv_det, cov_a * inv_det]
-    zero = jnp.zeros_like(rel_x)
-    one = jnp.ones_like(rel_x)
-    for channel in range(3):
-        out += pull([one if i == channel else zero for i in range(3)])
-    out += [jnp.where(x > 0.0, 1.0, jnp.where(x == 0.0, 0.5, 0.0)) for x in raw]
-    out += basis[1:]
     for i, x in enumerate(out):
         kept[i] = x
+    inv_dist = 1.0 / jnp.sqrt(rel_x * rel_x + rel_y * rel_y + means[2] * means[2])
+    turn = [rel_x * inv_dist, rel_y * inv_dist, means[2] * inv_dist]
+    basis = sh_basis(*turn)
+    slopes = basis_slopes(*turn)
+    for k in range(1, SH):
+        kept[26 + k] = basis[k]
+    for channel in range(3):
+        raw = sh_c0 * par[:, channel * SH, :] + 0.5
+        slope = [None, None, None]
+        for k in range(1, SH):
+            coeff = par[:, channel * SH + k, :]
+            raw = raw + coeff * basis[k]
+            for i in range(3):
+                if k in slopes[i]:
+                    term = coeff * slopes[i][k]
+                    slope[i] = term if slope[i] is None else slope[i] + term
+        along = turn[0] * slope[0] + turn[1] * slope[1] + turn[2] * slope[2]
+        for i in range(3):
+            kept[15 + 3 * channel + i] = (slope[i] - turn[i] * along) * inv_dist
+        kept[24 + channel] = jnp.where(raw > 0.0, 1.0, jnp.where(raw == 0.0, 0.5, 0.0))
 
 
 def pull_view(kept, cots, inv_depth, jac_diag, spread):
@@ -346,6 +393,34 @@
     d_diag = rel_x * d_ratio_u + rel_y * d_ratio_v
     d_inv = -(ratio_u * d_jac_u + ratio_v * d_jac_v)
     return d_top + d_low + d_base + [d_x, d_y, turn[2], d_diag, d_inv, cots[5]], shades
+
+
+def octets(x):
+    return [x[k : k + 8] for k in range(0, x.shape[0], 8)]
+
+
+def products_before(parts):
+    sub = lax.broadcasted_iota(jnp.int32, parts[0].shape, 0)
+    run, before = parts[0], [None]
+    for part in parts[1:]:
+        before.append(run)
+        run = run * part
+    lead = jnp.where(sub >= 1, pltpu.roll(run, 1, 0), 1.0)
+    for step in (1, 2, 4):
+        lead = lead * jnp.where(sub >= step, pltpu.roll(lead, step, 0), 1.0)
+    return [lead if x is None else x * lead for x in before]
+
+
+def sums_after(parts):
+    sub = lax.broadcasted_iota(jnp.int32, parts[0].shape, 0)
+    run, after = parts[-1], [None]
+    for part in parts[-2::-1]:
+        after.append(run)
+        run = run + part
+    tail = jnp.where(sub < 7, pltpu.roll(run, 7, 0), 0.0)
+    for step in (1, 2, 4):
+        tail = tail + jnp.where(sub < 8 - step, pltpu.roll(tail, 8 - step, 0), 0.0)
+    return [tail if x is None else x + tail for x in after[::-1]]
 
 
 def near_kernel(
@@ -386,11 +461,13 @@
     slot_mask_t,
     row_mask,
     bases,
+    bases_t,
     tile_buf,
     ratio_buf,
     weight_buf,
-    share_buf,
+    shade_buf,
     split_buf,
+    power_buf,
     pic,
     halo,
     t_halo,
@@ -571,14 +648,22 @@
     n_chunk, _, wide = weight_buf.shape
     width = tiles * TILE
     per = wide // width
+    deep = list_size // 8
+    place = lax.broadcasted_iota(jnp.int32, (list_size, list_size), 1)
+    moved = lax.broadcasted_iota(jnp.int32, (list_size, list_size), 0) == (
+        lax.rem(place, 8) * deep + place // 8
+    )
+    placed_lists = dot_exact(lists[...].astype(f32), jnp.where(moved, 1.0, 0.0))
+    placed_lists = jnp.floor(placed_lists + 0.5)
+    whole_lists = placed_lists.astype(jnp.int32)
     slot_row = lax.broadcasted_iota(jnp.int32, (cap, list_size), 0)
     for k in range(n_gs):
         here = slot_row + flip(gs, k) * cap
         for t in range(tiles):
             slot_mask[k, :, t * list_size : (t + 1) * list_size] = jnp.where(
-                here == lists[t : t + 1, :], 1.0, 0.0
+                here == whole_lists[t : t + 1, :], 1.0, 0.0
             ).astype(bf16)
-    lists_t = jnp.transpose(lists[...].astype(f32))
+    lists_t = jnp.transpose(placed_lists)
     slot_lane = lax.broadcasted_iota(jnp.int32, (list_size, cap), 1)
     for t in range(tiles):
         listed = jnp.broadcast_to(lists_t[:, t : t + 1], (list_size, cap))
@@ -595,12 +680,26 @@
     for i in range(n_chunk):
         off_r = half_r + float(i * per - TILE // 2)
         out = [jnp.ones_like(off_q), off_q, off_r, off_q * off_q, off_q * off_r, off_r * off_r]
-        bases[i] = jnp.concatenate([jnp.where(in_tile, x, 0.0) for x in out], axis=0).astype(bf16)
-    shape = (list_size, 2 * list_size)
-    list_row = lax.broadcasted_iota(jnp.int32, shape, 0)
-    list_col = lax.rem(lax.broadcasted_iota(jnp.int32, shape, 1), list_size)
-    prefix = jnp.where(list_col < list_row, 1.0, 0.0).astype(bf16)
-    suffix = jnp.where(list_col > list_row, 1.0, 0.0).astype(bf16)
+        base = jnp.concatenate([jnp.where(in_tile, x, 0.0) for x in out], axis=0)
+        bases[i] = base.astype(bf16)
+        bases_t[i * wide : (i + 1) * wide, :] = jnp.transpose(base).astype(bf16)
+    shape = (9 * tiles, 3 * width)
+    row_of, lane_of = [lax.broadcasted_iota(jnp.int32, shape, k) for k in range(2)]
+    at_tile = lax.rem(row_of, tiles) == lax.rem(lane_of, width) // TILE
+    at_channel = lax.rem(row_of // tiles, 3) == lane_of // width
+    widen = jnp.where(jnp.logical_and(at_tile, at_channel), 1.0, 0.0).astype(bf16)
+    p_means, p_quats, p_scales, p_opacity, _ = params(par, opacity)
+    spread, pull_spread = jax.vjp(spread_of, p_quats, p_scales)
+    inv_depth = 1.0 / p_means[2]
+    jac_diag = focal_length * inv_depth
+
+    def keep(h, j, of):
+        at = cams[of]
+        keep_view(
+            kept.at[h, j], par, spread, p_means, inv_depth, jac_diag, at[:, 0:1], at[:, 1:2]
+        )
+
+    keep(0, group, view)
     for t in range(tiles):
         tile_buf[t] = jnp.zeros((ROWS_MSG, list_size), f32)
 
@@ -620,6 +719,7 @@
     )
     used = jnp.sum(jnp.where(diagonal, lens[...].astype(f32), 0.0), axis=1, keepdims=True)
     entry = lax.broadcasted_iota(jnp.int32, (tiles, list_size), 1)
+    entry = lax.rem(entry, 8) * deep + entry // 8
     live = entry.astype(f32) < used
     mid_q = (lax.broadcasted_iota(jnp.int32, (tiles, list_size), 0) * TILE + TILE // 2).astype(f32)
     mid_r = (gs * TILE + TILE // 2).astype(f32)
@@ -641,27 +741,26 @@
     term_t = jnp.transpose(jnp.concatenate(pieces(jnp.concatenate(terms, axis=0), 3), axis=0))
     term_t = term_t.astype(bf16)
     colour = jnp.concatenate([tile_buf[:, 6 + c, :] for c in range(3)], axis=0)
-    col_hi, col_lo = pieces(colour, 2)
-    col_two = jnp.concatenate([col_hi, col_lo], axis=0)
-    col_wide = jnp.concatenate([col_two, col_two], axis=1).astype(bf16)
-    col_t = jnp.transpose(jnp.concatenate([col_hi, col_lo, col_hi], axis=0)).astype(bf16)
+    col_t = jnp.transpose(jnp.concatenate(pieces(colour, 3), axis=0)).astype(bf16)
+    shade_buf[...] = dot(col_t, widen)
 
     for i in range(n_chunk):
         base = bases[i]
         ratio_buf[i] = jnp.exp(dot(term_t, jnp.concatenate([base, base, base], axis=0)))
     for i in range(n_chunk):
-        alpha = ratio_buf[i]
-        weight = alpha * jnp.exp(dot(prefix, stack(jnp.log(1.0 - alpha), 2)))
-        weight_buf[i] = weight
-        split_buf[i] = stack(weight, 2)
-    for i in range(n_chunk):
-        drawn = fold(dot(col_wide, split_buf[i]), 2)
-        for c in range(3):
-            mine = jnp.where(in_tile, drawn[c * tiles : (c + 1) * tiles], 0.0)
-            line = jnp.sum(mine, axis=0, keepdims=True)
-            for half in range(per):
-                row = i * per + half
-                pic[c, row : row + 1, :] = line[:, half * width : (half + 1) * width]
+        for half in range(per):
+            lanes = slice(half * width, (half + 1) * width)
+            alpha = octets(ratio_buf[i, :, lanes])
+            before = products_before([1.0 - x for x in alpha])
+            weight = [x * y for x, y in zip(alpha, before)]
+            weight_buf[i, :, lanes] = jnp.concatenate(weight, axis=0)
+            row = i * per + half
+            for c in range(3):
+                shade = octets(shade_buf[:, c * width : (c + 1) * width])
+                total = weight[0] * shade[0]
+                for x, y in zip(weight[1:], shade[1:]):
+                    total = total + x * y
+                pic[c, row : row + 1, :] = jnp.sum(total, axis=0, keepdims=True)
 
     exchange(pic, halo, send_halo, recv_halo, True)
     pic_out[0] = pic[...]
@@ -693,8 +792,16 @@
             (1.0 - ssim_weight) / (TILE * TILE) * res / jnp.sqrt(res * res + charb_eps)
         )
     for i in range(n_chunk):
-        alpha = ratio_buf[i]
-        ratio_buf[i] = alpha / (1.0 - alpha)
+        split_buf[i] = stack(jnp.transpose(weight_buf[i]), 2, 1)
+        for half in range(per):
+            lanes = slice(half * width, (half + 1) * width)
+            alpha = ratio_buf[i, :, lanes]
+            ratio = alpha / (1.0 - alpha)
+            weight = weight_buf[i, :, lanes]
+            for c in range(3):
+                share = weight * shade_buf[:, c * width : (c + 1) * width]
+                after = jnp.concatenate(sums_after(octets(share)), axis=0)
+                power_buf[c, i, :, lanes] = share - ratio * after
     exchange(pic, halo, send_halo, recv_halo, False)
 
     beyond = []
@@ -728,34 +835,27 @@
         d_xx = -ssim * inv_dd
         d_xy = 2.0 * top_a * inv_cd
         cots += [jnp.where(inside, scale * part, 0.0) for part in (d_mean, d_xx, d_xy)]
-    spread = dot(band_back, stack_mixed(jnp.concatenate(cots, axis=1), 0))
-    spread = dot(stack_mixed(side_by_side(spread, 9), 1), across)
+    spread_rows = dot(band_back, stack_mixed(jnp.concatenate(cots, axis=1), 0))
+    spread_rows = dot(stack_mixed(side_by_side(spread_rows, 9), 1), across)
     grad_rows = []
     for c in range(3):
-        s_mean, s_xx, s_xy = [spread[(3 * c + i) * TILE : (3 * c + i + 1) * TILE] for i in range(3)]
+        s_mean, s_xx, s_xy = [spread_rows[(3 * c + i) * TILE : (3 * c + i + 1) * TILE] for i in range(3)]
         grad_rows.append(directs[c] + s_mean + 2.0 * pic[c] * s_xx + targets[0, c] * s_xy)
 
-    shades = []
+    d_terms = jnp.zeros((2 * list_size, 6 * tiles), f32)
+    d_colour = jnp.zeros((6 * tiles, 2 * list_size), f32)
     for i in range(n_chunk):
-        parts = []
-        for c in range(3):
-            line = jnp.concatenate(
+        lines = [
+            jnp.concatenate(
                 [grad_rows[c][i * per + half : i * per + half + 1] for half in range(per)], axis=1
             )
-            parts.append(jnp.where(in_tile, line, 0.0))
-        hi, lo = pieces(jnp.concatenate(parts, axis=0), 2)
-        shades.append(jnp.concatenate([hi, lo], axis=0).astype(bf16))
-        shade = dot(col_t, jnp.concatenate([hi, hi, lo], axis=0).astype(bf16))
-        share_buf[i] = weight_buf[i] * shade
-    for i in range(n_chunk):
-        share = share_buf[i]
-        share_buf[i] = share - ratio_buf[i] * dot(suffix, stack(share, 2))
-    d_terms = jnp.zeros((6 * tiles, 2 * list_size), f32)
-    d_colour = jnp.zeros((6 * tiles, 2 * list_size), f32)
-    for i in range(n_chunk):
-        d_terms = d_terms + dot_t(bases[i], stack(share_buf[i], 2))
-        d_colour = d_colour + dot_t(shades[i], split_buf[i])
-    d_terms = d_terms[:, :list_size] + d_terms[:, list_size:]
+            for c in range(3)
+        ]
+        shades = stack(jnp.concatenate([jnp.where(in_tile, x, 0.0) for x in lines], axis=0), 2)
+        d_power = lines[0] * power_buf[0, i] + lines[1] * power_buf[1, i] + lines[2] * power_buf[2, i]
+        d_terms = d_terms + dot(stack(d_power, 2), bases_t[i * wide : (i + 1) * wide, :])
+        d_colour = d_colour + dot(shades, split_buf[i])
+    d_terms = jnp.transpose(fold(d_terms, 2))
     d_colour = fold(d_colour[:, :list_size] + d_colour[:, list_size:], 2)
 
     d0, d1, d2, d3, d4, d5 = [d_terms[k * tiles : (k + 1) * tiles] for k in range(6)]
@@ -807,30 +907,23 @@
         row_mask[s] = jnp.where(shard_lane == send_t[:, s : s + 1], 1.0, 0.0).astype(bf16)
     for k in range(1, n_view):
         cam_copy(view, lax.rem(view + n_view - k, n_view)).wait_recv()
-    p_means, p_quats, p_scales, p_opacity, p_coeffs = params(par, opacity)
-    spread, pull_spread = jax.vjp(spread_of, p_quats, p_scales)
-    inv_depth = 1.0 / p_means[2]
-    jac_diag = focal_length * inv_depth
-    for h in range(2):
-        for j in range(groups):
-            of = 2 * j + (core if h == 0 else 1 - core)
-            at = cams[of]
-            keep_view(
-                kept.at[h, j], p_coeffs, spread, p_means, inv_depth, jac_diag, at[:, 0:1], at[:, 1:2]
-            )
-
-    placed[...] = jnp.zeros_like(placed)
-
-    def put_back(s):
+    for j in range(1, groups):
+        keep(0, lax.div(cousin(j), 2), cousin(j))
+    for j in range(groups):
+        keep(1, j, 2 * j + 1 - core)
+
+
+    def put_back(s, first):
         both = [stack(pad_rows(back_in[j, s]), 2) for j in range(groups)]
-        placed[...] += dot(jnp.concatenate(both, axis=0), row_mask[s])
+        got = dot(jnp.concatenate(both, axis=0), row_mask[s])
+        placed[...] = got if first else placed[...] + got
 
     for k in range(n_gs):
         s = flip(gs, k)
         for j in range(groups):
             if k or j:
                 in_copy(j, s).wait_recv()
-        put_back(s)
+        put_back(s, k == 0)
     for j in range(groups):
         mine = fold(placed[2 * ROWS_MSG * j : 2 * ROWS_MSG * (j + 1)], 2)
         for c in range(chunks):
@@ -1573,11 +1666,13 @@
             VMEM((n_gs, tiles * list_size, cap), bf16),
             VMEM((n_gs, cap, shard), bf16),
             VMEM((n_chunk, 6 * tiles, wide), bf16),
+            VMEM((n_chunk * wide, 6 * tiles), bf16),
             VMEM((tiles, ROWS_MSG, list_size), f32),
             VMEM((n_chunk, list_size, wide), f32),
             VMEM((n_chunk, list_size, wide), f32),
-            VMEM((n_chunk, list_size, wide), f32),
-            VMEM((n_chunk, 2 * list_size, wide), bf16),
+            VMEM((list_size, 3 * width), f32),
+            VMEM((n_chunk, wide, 2 * list_size), bf16),
+            VMEM((3, n_chunk, list_size, wide), f32),
             VMEM((3, TILE, width), f32),
             VMEM((2, 3, TILE, width), f32),
             VMEM((2, 3, TILE, width), f32),

time: 27.1 us -> 25 us (0.923)
  Pallas kernels: 26.3 us -> 24.2 us
    pallas_call x1, Pallas kernels: 25.5 us -> 23.5 us  [shards(): pl.pallas_call(lambda *refs: near_kernel(n_gs, n_view, *refs), out_shape=...]
where the time goes in v2:
time: 25 us; the launch traced here: 24.9 us
  Pallas kernels  24.2 us (97%)
  between operations  0.64 us (3%)
    pallas_call x1, Pallas kernels, shards(): pl.pallas_call(lambda *refs: near_kernel(n_gs, n_view, *refs), out_shape=...  23.5 us
    pallas_call x1, Pallas kernels, shards(): pl.pallas_call(store_kernel, out_shape=out_shape, in_specs=[vmem] * 6, ou...  0.76 us

profile of v2, /device:TPU:1, one launch (start us, length us, event | category | flops | bytes accessed | tf_op | source)
XLA Modules:
  0.0 24.9 jit_solution(4598564154603548771)
XLA Ops:
  0.6 23.5 %shard_map.145 = (f32[1,3,16,128]{3,2,1,0:T(8,128)S(1)}, f32[3,1024]{1,0:T(4,128)S(1)}, f32[4,1024]{1,0:T(4,128)S(1)}, f32[3,1024]{1,0:T(4,128)S(1)}, f32[8,128]{1,0:T(8,128)S(1)}, /*index=5*/f32[48,1024]{1,0:T(8,128)S(1)}) custom-call(f32[3,1024]{1,0:T(4,128)} %refs_0_.1, f32[4,1024]{1,0:T(4,128)} %refs_1_.1, f32[3,1024]{1,0:T(4,128)} %refs_2_.1, ...), custom_call_target="tpu_custom_call" | custom-call | tf_op jit(solution)/shard_map/pallas_call | solution.py:1644
  24.1 0.8 %shard_map.146 = (f32[1,3,16,128]{3,2,1,0:T(8,128)}, f32[3,1024]{1,0:T(4,128)}, f32[4,1024]{1,0:T(4,128)}, f32[3,1024]{1,0:T(4,128)}, f32[8,128]{1,0:T(8,128)}, /*index=5*/f32[48,1024]{1,0:T(8,128)}) custom-call(f32[1,3,16,128]{3,2,1,0:T(8,128)S(1)} %get-tuple-element.18.refs_0_, f32[3,1024]{1,0:T(4,128)S(1)} %get-tuple-element.19.refs_1_, ...), custom_call_target="tpu_custom_call" | custom-call | tf_op jit(solution)/shard_map/pallas_call | solution.py:1705

commit v3 on v2

--- a/solution.py
+++ b/solution.py
@@ -493,6 +493,36 @@
     send_three,
     recv_three,
 ):
+    gs = lax.axis_index("gs")
+    view = lax.axis_index("view")
+    shard = means.shape[1]
+    chunks = shard // LANES
+    cap = send.shape[2]
+    tiles, list_size = lists.shape
+    groups = n_view // 2
+    core = lax.rem(view, 2)
+    group = lax.div(view, 2)
+    has_up = gs > 0
+    has_down = gs < n_gs - 1
+    near = range(1, n_gs)
+    far = range(n_gs - 1, 0, -1)
+
+    def cousin(j):
+        return lax.rem(view + 2 * j, n_view)
+
+    barrier = pltpu.get_barrier_semaphore()
+
+    def greet(strip, cam):
+        pl.semaphore_signal(barrier, inc=1, device_id=(strip, cam), device_id_type=MESH)
+
+    for k in range(n_gs - 1, -1, -1):
+        for j in range(groups):
+            if k or j:
+                greet(flip(gs, k), cousin(j))
+    for j in range(groups):
+        greet(gs, flip(cousin(j), 1))
+    greeted = n_gs - 1 + (groups - 1) * n_gs + groups
+
     loads = [
         pltpu.make_async_copy(src, dst, load_sems.at[k])
         for k, (src, dst) in enumerate(
@@ -512,36 +542,6 @@
     ]
     for load in loads:
         load.start()
-    gs = lax.axis_index("gs")
-    view = lax.axis_index("view")
-    shard = means.shape[1]
-    chunks = shard // LANES
-    cap = send.shape[2]
-    tiles, list_size = lists.shape
-    groups = n_view // 2
-    core = lax.rem(view, 2)
-    group = lax.div(view, 2)
-    has_up = gs > 0
-    has_down = gs < n_gs - 1
-    near = range(1, n_gs)
-    far = range(n_gs - 1, 0, -1)
-
-    def cousin(j):
-        return lax.rem(view + 2 * j, n_view)
-
-    barrier = pltpu.get_barrier_semaphore()
-
-    def greet(strip, cam):
-        pl.semaphore_signal(barrier, inc=1, device_id=(strip, cam), device_id_type=MESH)
-
-    for k in near:
-        greet(flip(gs, k), view)
-    for j in range(1, groups):
-        for k in range(n_gs):
-            greet(flip(gs, k), cousin(j))
-    for j in range(groups):
-        greet(gs, flip(cousin(j), 1))
-    greeted = n_gs - 1 + (groups - 1) * n_gs + groups
 
     for load in loads[:7]:
         load.wait()
@@ -576,10 +576,11 @@
             device_id_type=MESH,
         )
 
-    pl.semaphore_wait(barrier, greeted)
-
     for k in far:
         fill(flip(gs, k))
+    pl.semaphore_wait(barrier, greeted)
+
+    for k in far:
         first_copy(flip(gs, k), gs).start()
     fill(gs)
     msg_in[gs] = msg_out[gs]

time: 25 us -> 24.3 us (0.972)
  Pallas kernels: 24.2 us -> 23.5 us
    pallas_call x1, Pallas kernels: 23.5 us -> 22.8 us  [shards(): pl.pallas_call(lambda *refs: near_kernel(n_gs, n_view, *refs), out_shape=...]
where the time goes in v3:
time: 24.3 us; the launch traced here: 24.2 us
  Pallas kernels  23.5 us (97%)
  between operations  0.64 us (3%)
    pallas_call x1, Pallas kernels, shards(): pl.pallas_call(lambda *refs: near_kernel(n_gs, n_view, *refs), out_shape=...  22.8 us
    pallas_call x1, Pallas kernels, shards(): pl.pallas_call(store_kernel, out_shape=out_shape, in_specs=[vmem] * 6, ou...  0.76 us

profile of v3, /device:TPU:1, one launch (start us, length us, event | category | flops | bytes accessed | tf_op | source)
XLA Modules:
  0.0 24.2 jit_solution(1794708293354359794)
XLA Ops:
  0.6 22.8 %shard_map.145 = (f32[1,3,16,128]{3,2,1,0:T(8,128)S(1)}, f32[3,1024]{1,0:T(4,128)S(1)}, f32[4,1024]{1,0:T(4,128)S(1)}, f32[3,1024]{1,0:T(4,128)S(1)}, f32[8,128]{1,0:T(8,128)S(1)}, /*index=5*/f32[48,1024]{1,0:T(8,128)S(1)}) custom-call(f32[3,1024]{1,0:T(4,128)} %refs_0_.1, f32[4,1024]{1,0:T(4,128)} %refs_1_.1, f32[3,1024]{1,0:T(4,128)} %refs_2_.1, ...), custom_call_target="tpu_custom_call" | custom-call | tf_op jit(solution)/shard_map/pallas_call | solution.py:1645
  23.4 0.8 %shard_map.146 = (f32[1,3,16,128]{3,2,1,0:T(8,128)}, f32[3,1024]{1,0:T(4,128)}, f32[4,1024]{1,0:T(4,128)}, f32[3,1024]{1,0:T(4,128)}, f32[8,128]{1,0:T(8,128)}, /*index=5*/f32[48,1024]{1,0:T(8,128)}) custom-call(f32[1,3,16,128]{3,2,1,0:T(8,128)S(1)} %get-tuple-element.18.refs_0_, f32[3,1024]{1,0:T(4,128)S(1)} %get-tuple-element.19.refs_1_, ...), custom_call_target="tpu_custom_call" | custom-call | tf_op jit(solution)/shard_map/pallas_call | solution.py:1706

commit v4 on v3

--- a/solution.py
+++ b/solution.py
@@ -510,6 +510,10 @@
     def cousin(j):
         return lax.rem(view + 2 * j, n_view)
 
+    reach = 2 * RADIUS
+    halo[...] = jnp.zeros_like(halo)
+    t_halo[...] = jnp.zeros_like(t_halo)
+
     barrier = pltpu.get_barrier_semaphore()
 
     def greet(strip, cam):
@@ -602,9 +606,10 @@
 
     def halo_copy(src, dst, sends, recvs, side):
         other = gs + 1 if side == 0 else gs - 1
+        rows = pl.ds(TILE - reach if side == 0 else 0, reach)
         return pltpu.make_async_remote_copy(
-            src_ref=src,
-            dst_ref=dst.at[side],
+            src_ref=src.at[:, rows],
+            dst_ref=dst.at[side, :, rows],
             send_sem=sends.at[side],
             recv_sem=recvs.at[side],
             device_id=(other, view),
@@ -635,16 +640,6 @@
     for load in loads[7:]:
         load.wait()
     exchange(targets.at[0], t_halo, send_tgt, recv_tgt, True)
-
-    @pl.when(jnp.logical_not(has_up))
-    def _():
-        halo[0] = jnp.zeros_like(halo[0])
-        t_halo[0] = jnp.zeros_like(t_halo[0])
-
-    @pl.when(jnp.logical_not(has_down))
-    def _():
-        halo[1] = jnp.zeros_like(halo[1])
-        t_halo[1] = jnp.zeros_like(t_halo[1])
 
     n_chunk, _, wide = weight_buf.shape
     width = tiles * TILE

time: 24.3 us -> 24.2 us (level)
  no operation moved by 1% of the time
where the time goes in v4:
time: 24.2 us; the launch traced here: 24.1 us
  Pallas kernels  23.4 us (97%)
  between operations  0.64 us (3%)
    pallas_call x1, Pallas kernels, shards(): pl.pallas_call(lambda *refs: near_kernel(n_gs, n_view, *refs), out_shape=...  22.7 us
    pallas_call x1, Pallas kernels, shards(): pl.pallas_call(store_kernel, out_shape=out_shape, in_specs=[vmem] * 6, ou...  0.76 us

profile of v4, /device:TPU:1, one launch (start us, length us, event | category | flops | bytes accessed | tf_op | source)
XLA Modules:
  0.0 24.1 jit_solution(8027220092173421504)
XLA Ops:
  0.6 22.7 %shard_map.145 = (f32[1,3,16,128]{3,2,1,0:T(8,128)S(1)}, f32[3,1024]{1,0:T(4,128)S(1)}, f32[4,1024]{1,0:T(4,128)S(1)}, f32[3,1024]{1,0:T(4,128)S(1)}, f32[8,128]{1,0:T(8,128)S(1)}, /*index=5*/f32[48,1024]{1,0:T(8,128)S(1)}) custom-call(f32[3,1024]{1,0:T(4,128)} %refs_0_.1, f32[4,1024]{1,0:T(4,128)} %refs_1_.1, f32[3,1024]{1,0:T(4,128)} %refs_2_.1, ...), custom_call_target="tpu_custom_call" | custom-call | tf_op jit(solution)/shard_map/pallas_call | solution.py:1640
  23.3 0.8 %shard_map.146 = (f32[1,3,16,128]{3,2,1,0:T(8,128)}, f32[3,1024]{1,0:T(4,128)}, f32[4,1024]{1,0:T(4,128)}, f32[3,1024]{1,0:T(4,128)}, f32[8,128]{1,0:T(8,128)}, /*index=5*/f32[48,1024]{1,0:T(8,128)}) custom-call(f32[1,3,16,128]{3,2,1,0:T(8,128)S(1)} %get-tuple-element.18.refs_0_, f32[3,1024]{1,0:T(4,128)S(1)} %get-tuple-element.19.refs_1_, ...), custom_call_target="tpu_custom_call" | custom-call | tf_op jit(solution)/shard_map/pallas_call | solution.py:1701
